TPU v7x, 512 devices: a whole 4x4x16 slice. The times are simulated.
512 devices in a mesh: grp: 8 (over y, x_lo), feat: 64 (over z, x_hi, core).
Axes of the slice: x: 4 (x_hi: 2, x_lo: 2; x = x_hi * 2 + x_lo), y: 4, z: 16, core: 2. Of those that a mesh axis runs over, the one named last changes fastest.
Arguments:
- grads: float32 [8, 512, 16384], P('grp', None, 'feat'), may hold values from -16 to 16
- partner: int32 [8, 2], replicated, may hold values from 0 to 511, as said below
Outputs:
- self_tile: float32 [8, 512, 512], P('grp', 'feat')
- cross_tile_t: float32 [8, 512, 512], P('grp', 'feat')
Inputs may be any that keep to these rules, and one draw needn't show every extreme that they name: partner[g,0] is a group other than g; partner[g,1] is a row offset, different for different groups.
All inputs are finite; a program needn't handle non-finite values.
Results may differ from a plain program's by a relative error of at most 0.0003.
Values sent between devices are 32-bit elements; how exact they have to be, the bound alone decides.
No kernel may reach another device: no remote copies, remote signals or barrier semaphores. Data moves between devices by JAX's collectives and lax.ppermute only.
A program may use at most 64 MiB of HBM per device.

v0:
```python
import math

import jax
import jax.numpy as jnp
from jax import lax
from jax.sharding import PartitionSpec as P

K = 16384


def local(grads, partner):
    own_rows = grads[0]
    row_count = own_rows.shape[0]
    own_group = lax.axis_index("grp")
    mate_group = partner[own_group, 0]
    mate_offset = partner[own_group, 1]
    scale = 1.0 / math.sqrt(K)
    piece = lax.all_gather(grads, "grp", axis=0, tiled=True)
    start = jnp.int32(0)
    count = piece.shape[0]
    offset = jnp.clip(mate_group, 0, count - 1)
    chosen = lax.dynamic_index_in_dim(piece, offset, 0, keepdims=False)
    inside = jnp.logical_and(mate_group >= start, mate_group < start + count)
    fetched = jnp.where(inside, chosen, jnp.zeros_like(own_rows))
    doubled = jnp.concatenate([fetched, fetched], axis=0)
    mate_rows = lax.dynamic_slice_in_dim(doubled, mate_offset, row_count, 0)
    self_term = jnp.dot(
        own_rows, own_rows.T, preferred_element_type=jnp.float32, precision=lax.Precision.HIGHEST
    )
    cross_term = jnp.dot(
        mate_rows, own_rows.T, preferred_element_type=jnp.float32, precision=lax.Precision.HIGHEST
    )
    stacked = lax.psum_scatter(
        jnp.concatenate([self_term, cross_term], axis=1), "feat", scatter_dimension=0, tiled=True
    )
    self_mine = stacked[:, :row_count]
    cross_mine = stacked[:, row_count:]
    return ((self_mine * scale)[None], (cross_mine * scale)[None])


def solution(mesh):
    in_specs = (P("grp", None, "feat"), P())
    out_specs = (P("grp", "feat", None), P("grp", "feat", None))
    return jax.shard_map(local, mesh=mesh, in_specs=in_specs, out_specs=out_specs, check_vma=False)
```

profile of v0, /device:TPU:6, one launch (start us, length us, event | category | flops | bytes accessed | tf_op | source)
XLA Modules:
  0.0 340.1 jit_solution(3078663601420487157)
XLA Ops:
  7.2 0.0 copy-start
  7.2 0.0 all-gather.2.cloned.1.call-start
  7.2 0.7 all-gather.2.cloned.1.call-update
  7.9 0.0 reduce-scatter.4.cloned.1.call-start
  8.0 1.3 constant_dynamic-slice_fusion
  13.2 2.3 fusion.4
  15.5 96.8 %all-gather.2.cloned.1.call-done = f32[8,512,256]{2,1,0:T(8,128)} async-done(((f32[1,512,256]{2,1,0:T(8,128)}), f32[8,512,256]{2,1,0:T(8,128)}) %all-gather.2.cloned.1.call-update) | async-done | bytes 4194320 | tf_op jit(solution)/shard_map/all_gather | solution.py:18
  112.2 1.1 select_bitcast_fusion
  113.3 0.0 copy-done
  113.3 1.2 fusion.1
  114.5 0.2 pad_maximum_fusion
  114.7 1.9 copy.8
  116.6 0.0 reduce-scatter.4.cloned.1.call-update
  116.6 214.2 %reduce-scatter.4.cloned.1.call-done = f32[8,1024]{1,0:T(8,128)} async-done(((f32[512,1024]{1,0:T(8,128)}), f32[8,1024]{1,0:T(8,128)}) %reduce-scatter.4.cloned.1.call-update) | async-done | bytes 32784
  330.8 0.7 fusion.8
  331.5 0.1 copy.11
  331.7 0.7 copy.7
  332.4 0.1 copy.10
  332.5 0.7 copy.6
  (2 shorter events, 0.0 us)
Async XLA Ops:
  7.2 106.1 %copy-start = (f32[1,512,256]{2,1,0:T(8,128)S(1)}, f32[1,512,256]{2,1,0:T(8,128)}, u32[]{:S(2)}) copy-start(f32[1,512,256]{2,1,0:T(8,128)} %param.2) | copy-start | bytes 1572868
  7.2 105.0 %all-gather.2.cloned.1.call-start = ((), (), s32[]{:S(2)}) async-start(), calls=%async_computation.1 | async-start | bytes 4718592 | tf_op jit(solution)/shard_map/all_gather | solution.py:18
  7.9 322.9 %reduce-scatter.4.cloned.1.call-start = ((), (), s32[]{:S(2)}) async-start(), calls=%async_computation.2 | async-start | bytes 2129920
Sparse Core Ops, SparseCore 0:
  10.1 102.0 all-gather.1
  116.9 213.8 reduce-scatter.3
where the time goes:
time: 342 us; the launch traced here: 340 us
  waiting for transfers between devices  312 us (91%)
  between operations  18 us (5%)
  local copies, waits for them, and re-layouts  5.63 us (2%)
  matrix products  3.47 us (1%)
    unnamed x3, waiting for transfers between devices  215 us
    all_gather x1, waiting for transfers between devices, local(): piece = lax.all_gather(grads, 'grp', axis=0, tiled=True)  96.8 us
  transfers between devices with their start and end apart: 2, of which 2 were waited for; matrix products, arithmetic and copies ran while one was open for 1% of the time, Pallas kernels for 0%

commit v1 on v0

v1 whole, which is shorter than its diff:
```python
import math

import jax
import jax.numpy as jnp
from jax import lax
from jax.experimental import pallas as pl
from jax.experimental.pallas import tpu as pltpu
from jax.sharding import Mesh, PartitionSpec as P

K = 16384
ROWS = 512
GROUPS = 8
FEATS = 256
Z = 16
QUADS = 4
BAND = 32
RUN = 8
SWAP = [(0, 1), (1, 0)]
NEAR = (0, 2, 1, 3)


def route_kernel(partner_ref, rows_ref, out_ref):
    for g in range(GROUPS):
        mate = partner_ref[g, 0]
        turn = lax.rem(BAND - lax.rem(partner_ref[g, 1], BAND), BAND)
        for v in range(2):
            band = rows_ref[mate, pl.ds(v * BAND, BAND), :]
            band = pltpu.roll(band, turn, 0)
            for q in range(QUADS):
                out_ref[g, q, v] = band[q * RUN : (q + 1) * RUN]


def route(partner, rows):
    return pl.pallas_call(
        route_kernel,
        out_shape=jax.ShapeDtypeStruct((GROUPS, QUADS, 2, RUN, FEATS), jnp.float32),
        in_specs=[pl.BlockSpec(memory_space=pltpu.SMEM), pl.BlockSpec(memory_space=pltpu.VMEM)],
        out_specs=pl.BlockSpec(memory_space=pltpu.VMEM),
        name="route",
    )(partner, rows)


def tiles_kernel(where_ref, own_ref, side_ref, cores_ref, mate_ref, out_ref, left_ref, acc_ref):
    quad = where_ref[0]
    shift = where_ref[1]
    turn = where_ref[2]
    lane_row = lax.broadcasted_iota(jnp.int32, (RUN, FEATS), 0)
    wrapped = lane_row + (turn + quad * RUN) >= BAND
    for i, near in enumerate(NEAR):
        block = (own_ref, side_ref, cores_ref.at[0], cores_ref.at[1])[i]
        source = quad ^ near
        for zo in range(Z):
            start = pl.multiple_of(zo * BAND + quad * RUN, RUN)
            left_ref[pl.ds(zo * RUN, RUN), :] = block[pl.ds(start, RUN), :]
            low = lax.rem(zo + shift, Z)
            high = lax.rem(zo + shift + 1, Z)
            near_rows = mate_ref[low // 2, source, low % 2]
            far_rows = mate_ref[high // 2, source, high % 2]
            left_ref[pl.ds((Z + zo) * RUN, RUN), :] = jnp.where(wrapped, far_rows, near_rows)
        part = lax.dot_general(
            left_ref[...],
            block[...],
            (((1,), (1,)), ((), ())),
            preferred_element_type=jnp.float32,
            precision=lax.Precision.HIGHEST,
        )
        if i == 0:
            acc_ref[...] = part
        elif i < 3:
            acc_ref[...] += part
        else:
            total = acc_ref[...] + part
            for t in range(2):
                for zo in range(Z):
                    at = (t * Z + zo) * RUN
                    out_ref[zo, t] = total[at : at + RUN]


def tiles(where, own, side, cores, mate):
    vmem = pl.BlockSpec(memory_space=pltpu.VMEM)
    return pl.pallas_call(
        tiles_kernel,
        out_shape=jax.ShapeDtypeStruct((Z, 2, RUN, ROWS), jnp.float32),
        in_specs=[pl.BlockSpec(memory_space=pltpu.SMEM), vmem, vmem, vmem, vmem],
        out_specs=vmem,
        scratch_shapes=[
            pltpu.VMEM((2 * Z * RUN, FEATS), jnp.float32),
            pltpu.VMEM((2 * Z * RUN, ROWS), jnp.float32),
        ],
        compiler_params=pltpu.CompilerParams(vmem_limit_bytes=32 << 20),
        name="tiles",
    )(where, own, side, cores, mate)


def local(grads, partner):
    own = grads[0]
    group = lax.axis_index("grp")
    quad = lax.axis_index("xh") * 2 + lax.axis_index("core")
    offset = partner[group, 1]
    where = jnp.stack([quad, offset // BAND, offset % BAND]).astype(jnp.int32)

    side = lax.ppermute(own, "xh", SWAP)
    chunks = lax.all_to_all(own.reshape(GROUPS, ROWS // GROUPS, FEATS), "grp", 0, 0)
    cores = lax.ppermute(jnp.stack([own, side]), "core", SWAP)
    routed = route(partner, chunks)
    mate = lax.all_to_all(
        routed.reshape(GROUPS * QUADS, 2, RUN, FEATS), ("grp", "xh", "core"), 0, 0
    ).reshape(GROUPS, QUADS, 2, RUN, FEATS)
    terms = tiles(where, own, side, cores, mate)
    scale = 1.0 / math.sqrt(K)
    total = jnp.sum(lax.all_to_all(terms, "z", 0, 0), axis=0) * scale
    return total[0][None], total[1][None]


def solution(mesh):
    axes = ("grp", "z", "xh", "core")
    fine = Mesh(mesh.devices.reshape(GROUPS, Z, 2, 2), axes)
    feat = ("z", "xh", "core")
    in_specs = (P("grp", None, feat), P())
    out_specs = (P("grp", feat, None), P("grp", feat, None))
    return jax.shard_map(local, mesh=fine, in_specs=in_specs, out_specs=out_specs, check_vma=False)
```

time: 342 us -> 105 us (0.31)
  the two profiles are of different devices: /device:TPU:6 before, /device:TPU:32 now
where the time goes in v1:
time: 105 us; the launch traced here: 104 us
  blocking collectives  44.9 us (43%)
  waiting for transfers between devices  30.4 us (29%)
  starting transfers between devices  17 us (16%)
  Pallas kernels  4.95 us (5%)
  between operations  3.31 us (3%)
  local copies, waits for them, and re-layouts  2.67 us (3%)
  other arithmetic  1.23 us (1%)
    all_to_all x1, blocking collectives, local(): total = jnp.sum(lax.all_to_all(terms, 'z', 0, 0), axis=0) * scale  44.9 us
    ppermute x1, waiting for transfers between devices, local(): side = lax.ppermute(own, 'xh', SWAP)  12.3 us
    all_to_all x1, waiting for transfers between devices, local(): lax.all_to_all(own.reshape(GROUPS, ROWS // GROUPS, FEATS), 'grp', 0, 0)  10.1 us
    all_to_all x1, waiting for transfers between devices, local(): lax.all_to_all(routed.reshape(GROUPS * QUADS, 2, RUN, FEATS), ('grp', 'xh...  7.95 us
    all_to_all x1, starting transfers between devices, local(): lax.all_to_all(own.reshape(GROUPS, ROWS // GROUPS, FEATS), 'grp', 0, 0)  5.41 us
    ppermute x1, starting transfers between devices, local(): side = lax.ppermute(own, 'xh', SWAP)  4.93 us
    all_to_all x1, starting transfers between devices, local(): lax.all_to_all(routed.reshape(GROUPS * QUADS, 2, RUN, FEATS), ('grp', 'xh...  4.69 us
    pallas_call x1, Pallas kernels, tiles(): pl.pallas_call(tiles_kernel, out_shape=jax.ShapeDtypeStruct((Z, 2, RUN, R...  3.02 us
  transfers between devices with their start and end apart: 4, of which 3 were waited for; matrix products, arithmetic and copies ran while one was open for 1% of the time, Pallas kernels for 2%

profile of v1, /device:TPU:32, one launch (start us, length us, event | category | flops | bytes accessed | tf_op | source)
XLA Modules:
  0.0 104.3 jit_solution(14825686059566277016)
XLA Ops:
  0.6 4.9 %collective-permute-start = (f32[512,256]{1,0:T(8,128)}, f32[512,256]{1,0:T(8,128)S(1)}, u32[]{:S(2)}, u32[]{:S(2)}) collective-permute-start(f32[512,256]{1,0:T(8,128)} %bitcast.4.own_ref), channel_id=1, source_target_pairs={{0,2},{2,0},{1,3},{3,1},{4,6},{6,4},{5,7},{7,5},{8,10},{10,8},{9,1... | collective-permute-start | bytes 1572872 | tf_op jit(solution)/shard_map/ppermute | solution.py:102
  5.6 12.3 %collective-permute-done.side_ref = f32[512,256]{1,0:T(8,128)S(1)} collective-permute-done((f32[512,256]{1,0:T(8,128)}, f32[512,256]{1,0:T(8,128)S(1)}, u32[]{:S(2)}, u32[]{:S(2)}) %collective-permute-start) | collective-permute-done | bytes 524320 | tf_op jit(solution)/shard_map/ppermute | solution.py:102
  17.9 1.1 %pad_maximum_fusion = f32[2,512,256]{2,1,0:T(8,128)S(1)} fusion(f32[1,512,256]{2,1,0:T(8,128)S(1)} %bitcast.10, f32[1,512,256]{2,1,0:T(8,128)} %param.2), kind=kLoop, calls=%fused_computation | loop fusion | flops 262144 | bytes 2097152 | tf_op jit(solution)/shard_map/stack | solution.py:104
  19.0 1.9 %collective-permute-start.1 = (f32[2,512,256]{2,1,0:T(8,128)S(1)}, f32[2,512,256]{2,1,0:T(8,128)S(1)}, u32[]{:S(2)}, u32[]{:S(2)}) collective-permute-start(f32[2,512,256]{2,1,0:T(8,128)S(1)} %pad_maximum_fusion), channel_id=1, source_target_pairs={{0,1},{1,0},{2,3},{3,2},{4,5},{5,4},{6,7},{7,6},{8,9},{9,8},{10,11... | collective-permute-start | bytes 3145736 | tf_op jit(solution)/shard_map/ppermute | solution.py:104
  20.9 0.0 copy-start.1
  21.0 5.4 %all-to-all-start = ((f32[8,64,256]{2,1,0:T(8,128)}), f32[8,64,256]{2,1,0:T(8,128)S(1)}, u32[]{:S(2)}, u32[]{:S(2)}) async-start(f32[8,64,256]{2,1,0:T(8,128)} %bitcast.6), calls=%async_computation | async-start | bytes 1048576 | tf_op jit(solution)/shard_map/all_to_all | solution.py:103
  26.4 0.0 copy-done.1
  26.4 0.7 copy.4.partner_ref
  27.0 10.1 %all-to-all-done.rows_ref = f32[8,64,256]{2,1,0:T(8,128)S(1)} async-done(((f32[8,64,256]{2,1,0:T(8,128)}), f32[8,64,256]{2,1,0:T(8,128)S(1)}, u32[]{:S(2)}, u32[]{:S(2)}) %all-to-all-start) | async-done | bytes 524320 | tf_op jit(solution)/shard_map/all_to_all | solution.py:103
  37.1 0.0 copy-start
  37.1 0.8 copy-done
  37.9 1.9 %route.1 = f32[8,4,2,8,256]{4,3,2,1,0:T(8,128)} custom-call(s32[8,2]{1,0:T(8,128)} %copy.4.partner_ref, f32[8,64,256]{2,1,0:T(8,128)} %copy-done), custom_call_target="tpu_custom_call" | custom-call | tf_op jit(solution)/shard_map/route/pallas_call | solution.py:34
  39.8 4.7 %all-to-all-start.1 = ((f32[32,2,8,256]{3,2,1,0:T(8,128)}), f32[32,2,8,256]{3,2,1,0:T(8,128)S(1)}, u32[]{:S(2)}, u32[]{:S(2)}) async-start(f32[32,2,8,256]{3,2,1,0:T(8,128)} %bitcast.11), calls=%async_computation.1 | async-start | bytes 1048576 | tf_op jit(solution)/shard_map/all_to_all | solution.py:106
  44.5 0.6 constant_dynamic-slice_fusion
  47.7 0.1 pad_add_fusion.where_ref
  47.8 8.0 %all-to-all-done.1 = f32[32,2,8,256]{3,2,1,0:T(8,128)S(1)} async-done(((f32[32,2,8,256]{3,2,1,0:T(8,128)}), f32[32,2,8,256]{3,2,1,0:T(8,128)S(1)}, u32[]{:S(2)}, u32[]{:S(2)}) %all-to-all-start.1) | async-done | bytes 524320 | tf_op jit(solution)/shard_map/all_to_all | solution.py:106
  55.8 0.0 collective-permute-done.1.cores_ref
  55.8 3.0 %tiles.1 = f32[16,2,8,512]{3,2,1,0:T(8,128)S(1)} custom-call(s32[3]{0:T(128)S(1)} %pad_add_fusion.where_ref, f32[512,256]{1,0:T(8,128)} %bitcast.4.own_ref, f32[512,256]{1,0:T(8,128)S(1)} %collective-permute-done.side_ref, f32[2,512,256]{2,1,0:T(8,128)S(1)} %collective-permute-done.1.cores_ref, f32[8,4,2,8,256]{4,3,2,1,0:T(8,128)S(1)} %bitcast.9), custom_call_target="tpu_custom_call" | custom-call | tf_op jit(solution)/shard_map/tiles/pallas_call | solution.py:81
  58.8 44.9 %all_to_all.15 = f32[16,2,8,512]{3,2,1,0:T(8,128)S(1)} all-to-all(f32[16,2,8,512]{3,2,1,0:T(8,128)S(1)} %tiles.1), channel_id=1, replica_groups=mesh['grp'=8,'z'=16,'xh'=2,'core'=2] {'z'}, dimensions={0} | all-to-all | bytes 1048576 | tf_op jit(solution)/shard_map/all_to_all | solution.py:111
  103.7 0.6 fusion
  (2 shorter events, 0.0 us)
Async XLA Ops:
  0.6 17.3 %collective-permute-start = (f32[512,256]{1,0:T(8,128)}, f32[512,256]{1,0:T(8,128)S(1)}, u32[]{:S(2)}, u32[]{:S(2)}) collective-permute-start(f32[512,256]{1,0:T(8,128)} %bitcast.4.own_ref), channel_id=1, source_target_pairs={{0,2},{2,0},{1,3},{3,1},{4,6},{6,4},{5,7},{7,5},{8,10},{10,8},{9,1... | collective-permute-start | bytes 1572872 | tf_op jit(solution)/shard_map/ppermute | solution.py:102
  19.0 36.8 %collective-permute-start.1 = (f32[2,512,256]{2,1,0:T(8,128)S(1)}, f32[2,512,256]{2,1,0:T(8,128)S(1)}, u32[]{:S(2)}, u32[]{:S(2)}) collective-permute-start(f32[2,512,256]{2,1,0:T(8,128)S(1)} %pad_maximum_fusion), channel_id=1, source_target_pairs={{0,1},{1,0},{2,3},{3,2},{4,5},{5,4},{6,7},{7,6},{8,9},{9,8},{10,11... | collective-permute-start | bytes 3145736 | tf_op jit(solution)/shard_map/ppermute | solution.py:104
  20.9 5.4 %copy-start.1 = (s32[8,2]{0,1:T(2,128)S(1)}, s32[8,2]{0,1:T(2,128)}, u32[]{:S(2)}) copy-start(s32[8,2]{0,1:T(2,128)} %param.3) | copy-start | bytes 196
  21.0 16.2 %all-to-all-start = ((f32[8,64,256]{2,1,0:T(8,128)}), f32[8,64,256]{2,1,0:T(8,128)S(1)}, u32[]{:S(2)}, u32[]{:S(2)}) async-start(f32[8,64,256]{2,1,0:T(8,128)} %bitcast.6), calls=%async_computation | async-start | bytes 1048576 | tf_op jit(solution)/shard_map/all_to_all | solution.py:103
  37.1 0.8 copy-start
  39.8 15.9 %all-to-all-start.1 = ((f32[32,2,8,256]{3,2,1,0:T(8,128)}), f32[32,2,8,256]{3,2,1,0:T(8,128)S(1)}, u32[]{:S(2)}, u32[]{:S(2)}) async-start(f32[32,2,8,256]{3,2,1,0:T(8,128)} %bitcast.11), calls=%async_computation.1 | async-start | bytes 1048576 | tf_op jit(solution)/shard_map/all_to_all | solution.py:106

commit v2 on v0

v2 whole, which is shorter than its diff:
```python
import math

import jax
import jax.numpy as jnp
from jax import lax
from jax.experimental import pallas as pl
from jax.experimental.pallas import tpu as pltpu
from jax.sharding import Mesh, PartitionSpec as P

K = 16384
ROWS = 512
GROUPS = 8
FEATS = 256
QUAD = 4
BANDS = 8
BAND = 64
RUN = 8
MINE = 128
SWAP = [(0, 1), (1, 0)]
NEAR = (0, 2, 1, 3)
HINT = 5_000_000_000
VMEM = pl.BlockSpec(memory_space=pltpu.VMEM)
SMEM = pl.BlockSpec(memory_space=pltpu.SMEM)


def call(kernel, shape, specs, arrays, limit, flops=0, scratch=()):
    def one(dims):
        return jax.ShapeDtypeStruct(dims, jnp.float32)

    several = isinstance(shape, list)
    return pl.pallas_call(
        kernel,
        out_shape=[one(dims) for dims in shape] if several else one(shape),
        in_specs=specs,
        out_specs=[VMEM] * len(shape) if several else VMEM,
        scratch_shapes=scratch,
        compiler_params=pltpu.CompilerParams(vmem_limit_bytes=limit << 20),
        cost_estimate=pl.CostEstimate(flops=flops, bytes_accessed=0, transcendentals=0),
        name=kernel.__name__,
    )(*arrays)


def run_of(member, xh):
    return member // 2 * 4 + xh * 2 + lax.rem(member, 2)


def route_kernel(partner_ref, rows_ref, out_ref):
    for g in range(GROUPS):
        turn = lax.rem(BAND - lax.rem(partner_ref[g, 1], BAND), BAND)
        band = pltpu.roll(rows_ref[partner_ref[g, 0]], turn, 0)
        for m in range(QUAD):
            for xh in range(2):
                at = (m // 2 * 4 + xh * 2 + m % 2) * RUN
                out_ref[g * QUAD + m, xh] = band[at : at + RUN]


def stack_kernel(own_ref, above_ref, near_ref):
    near_ref[0] = own_ref[...]
    near_ref[1] = above_ref[...]


def halves(values):
    high = values.astype(jnp.bfloat16)
    return high, (values - high.astype(jnp.float32)).astype(jnp.bfloat16)


def dot(left, right):
    return lax.dot_general(left, right, (((1,), (1,)), ((), ())), preferred_element_type=jnp.float32)


def products(blocks, rows_ref, fill):
    total = rest = None
    for i, block in enumerate(blocks):
        fill(i)
        rows_high, rows_low = halves(rows_ref[...])
        high, low = halves(block[...])
        part = dot(high, jnp.concatenate([rows_high, rows_low], axis=0))
        other = dot(low, rows_high)
        total = part if total is None else total + part
        rest = other if rest is None else rest + other
    return (total[:, :MINE] + total[:, MINE:] + rest).T


def blocks_of(near_ref, cores_ref):
    return [near_ref.at[0], near_ref.at[1], cores_ref.at[0], cores_ref.at[1]]


def member():
    return lax.axis_index("zl") * 2 + lax.axis_index("core")


def self_kernel(near_ref, cores_ref, out_ref, rows_ref):
    me = member()
    blocks = blocks_of(near_ref, cores_ref)

    def fill(i):
        for band in range(BANDS):
            for xh in range(2):
                start = pl.multiple_of(band * BAND + run_of(me, xh) * RUN, RUN)
                rows_ref[pl.ds((band * 2 + xh) * RUN, RUN), :] = blocks[i][pl.ds(start, RUN), :]

    out_ref[...] = products(blocks, rows_ref, fill)


def cross_kernel(partner_ref, near_ref, cores_ref, mate_ref, self_ref, out_ref, rows_ref):
    me = member()
    offset = partner_ref[lax.axis_index("grp"), 1]
    shift = offset // BAND
    row = lax.broadcasted_iota(jnp.int32, (RUN, FEATS), 0) + lax.rem(offset, BAND)

    def fill(i):
        source = me ^ NEAR[i]
        for band in range(BANDS):
            low = lax.rem(band + shift, BANDS) * QUAD + source
            high = lax.rem(band + shift + 1, BANDS) * QUAD + source
            for xh in range(2):
                rows_ref[pl.ds((band * 2 + xh) * RUN, RUN), :] = jnp.where(
                    row + run_of(me, xh) * RUN >= BAND, mate_ref[high, xh], mate_ref[low, xh]
                )

    cross = products(blocks_of(near_ref, cores_ref), rows_ref, fill)
    for band in range(BANDS):
        for xh in range(2):
            at = (band * 2 + xh) * RUN
            out_ref[band % 2 * 2 + xh, band // 2, 0] = self_ref[at : at + RUN]
            out_ref[band % 2 * 2 + xh, band // 2, 1] = cross[at : at + RUN]


def middle_kernel(terms_ref, out_ref):
    out_ref[...] = terms_ref[0] + terms_ref[1] + terms_ref[2] + terms_ref[3]


def total_kernel(terms_ref, self_ref, cross_ref):
    total = terms_ref[0]
    for i in range(1, terms_ref.shape[0]):
        total = total + terms_ref[i]
    total = total * (1.0 / math.sqrt(K))
    self_ref[0] = total[0]
    cross_ref[0] = total[1]


def local(grads, partner):
    own = grads[0]
    chunks = lax.all_to_all(own.reshape(GROUPS, BAND, FEATS), "grp", 0, 0)
    above = lax.ppermute(own, "zl", SWAP)
    routed = call(route_kernel, (GROUPS * QUAD, 2, RUN, FEATS), [SMEM, VMEM], (partner, chunks), 8)
    mate = lax.all_to_all(routed, ("grp", "zl", "core"), 0, 0)
    near = call(stack_kernel, (2, ROWS, FEATS), [VMEM, VMEM], (own, above), 8)
    cores = lax.ppermute(near, "core", SWAP)
    scratch = [pltpu.VMEM((MINE, FEATS), jnp.float32)]
    self_rows = call(self_kernel, (MINE, ROWS), [VMEM, VMEM], (near, cores), 12, HINT, scratch)
    terms = call(
        cross_kernel,
        (4, 4, 2, RUN, ROWS),
        [SMEM] + [VMEM] * 4,
        (partner, near, cores, mate, self_rows),
        12,
        0,
        scratch,
    )
    terms = lax.all_to_all(terms, ("zm", "xh"), 0, 0)
    terms = call(middle_kernel, (4, 2, RUN, ROWS), [VMEM], (terms,), 8)
    terms = lax.all_to_all(terms, "zo", 0, 0)
    return tuple(call(total_kernel, [(1, RUN, ROWS)] * 2, [VMEM], (terms,), 8))


def solution(mesh):
    fine = Mesh(mesh.devices.reshape(GROUPS, 4, 2, 2, 2, 2), ("grp", "zo", "zm", "zl", "xh", "core"))
    feat = ("zo", "zm", "zl", "xh", "core")
    in_specs = (P("grp", None, feat), P())
    out_specs = (P("grp", feat, None), P("grp", feat, None))
    return jax.shard_map(local, mesh=fine, in_specs=in_specs, out_specs=out_specs, check_vma=False)
```

time: 342 us -> 84.2 us (0.25)
  the two profiles are of different devices: /device:TPU:6 before, /device:TPU:1 now
where the time goes in v2:
time: 84.2 us; the launch traced here: 83.8 us
  blocking collectives  45.7 us (54%)
  starting transfers between devices  20.9 us (25%)
  waiting for transfers between devices  12 us (14%)
  Pallas kernels  4.48 us (5%)
    all_to_all x1, blocking collectives, local(): terms = lax.all_to_all(terms, 'zo', 0, 0)  24.3 us
    all_to_all x1, blocking collectives, local(): terms = lax.all_to_all(terms, ('zm', 'xh'), 0, 0)  21.4 us
    all_to_all x1, starting transfers between devices, local(): mate = lax.all_to_all(routed, ('grp', 'zl', 'core'), 0, 0)  9.06 us
    all_to_all x1, starting transfers between devices, local(): chunks = lax.all_to_all(own.reshape(GROUPS, BAND, FEATS), 'grp', 0, 0)  6.09 us
    all_to_all x1, waiting for transfers between devices, local(): mate = lax.all_to_all(routed, ('grp', 'zl', 'core'), 0, 0)  5.79 us
    pallas_call x6, Pallas kernels, call(): pl.pallas_call(kernel, out_shape=[one(dims) for dims in shape] if several...  4.48 us
    all_to_all x1, waiting for transfers between devices, local(): chunks = lax.all_to_all(own.reshape(GROUPS, BAND, FEATS), 'grp', 0, 0)  3.88 us
    ppermute x1, starting transfers between devices, local(): above = lax.ppermute(own, 'zl', SWAP)  3.55 us
  transfers between devices with their start and end apart: 4, of which 3 were waited for; matrix products, arithmetic and copies ran while one was open for 0% of the time, Pallas kernels for 3%

profile of v2, /device:TPU:1, one launch (start us, length us, event | category | flops | bytes accessed | tf_op | source)
XLA Modules:
  0.0 83.8 jit_solution(508606923531207460)
XLA Ops:
  0.6 0.0 copy-start
  0.6 6.1 %all-to-all-start = ((f32[8,64,256]{2,1,0:T(8,128)}), f32[8,64,256]{2,1,0:T(8,128)S(1)}, u32[]{:S(2)}, u32[]{:S(2)}) async-start(f32[8,64,256]{2,1,0:T(8,128)} %bitcast.2), calls=%async_computation | async-start | bytes 1048576 | tf_op jit(solution)/shard_map/all_to_all | solution.py:144
  6.7 0.0 copy-start.1
  6.7 0.0 copy-done
  6.7 3.5 %collective-permute-start = (f32[512,256]{1,0:T(8,128)S(1)}, f32[512,256]{1,0:T(8,128)S(1)}, u32[]{:S(2)}, u32[]{:S(2)}) collective-permute-start(f32[512,256]{1,0:T(8,128)S(1)} %bitcast.3), channel_id=1, source_target_pairs={{0,4},{4,0},{1,5},{5,1},{2,6},{6,2},{3,7},{7,3},{8,12},{12,8},{9,1... | collective-permute-start | bytes 1572872 | tf_op jit(solution)/shard_map/ppermute | solution.py:145
  10.3 0.0 copy-done.1
  10.3 0.1 copy.5.partner_ref
  10.4 3.9 %all-to-all-done.rows_ref = f32[8,64,256]{2,1,0:T(8,128)S(1)} async-done(((f32[8,64,256]{2,1,0:T(8,128)}), f32[8,64,256]{2,1,0:T(8,128)S(1)}, u32[]{:S(2)}, u32[]{:S(2)}) %all-to-all-start) | async-done | bytes 524320 | tf_op jit(solution)/shard_map/all_to_all | solution.py:144
  14.3 1.5 %route_kernel.1 = f32[32,2,8,256]{3,2,1,0:T(8,128)} custom-call(s32[8,2]{1,0:T(8,128)S(1)} %copy.5.partner_ref, f32[8,64,256]{2,1,0:T(8,128)S(1)} %all-to-all-done.rows_ref), custom_call_target="tpu_custom_call" | custom-call | tf_op jit(solution)/shard_map/route_kernel/pallas_call | solution.py:31
  15.8 9.1 %all-to-all-start.1 = ((f32[32,2,8,256]{3,2,1,0:T(8,128)}), f32[32,2,8,256]{3,2,1,0:T(8,128)S(1)}, u32[]{:S(2)}, u32[]{:S(2)}) async-start(f32[32,2,8,256]{3,2,1,0:T(8,128)} %route_kernel.1), calls=%async_computation.1 | async-start | bytes 1048576 | tf_op jit(solution)/shard_map/all_to_all | solution.py:147
  24.8 0.0 collective-permute-done.above_ref
  24.8 0.1 stack_kernel.1.near_ref
  24.9 2.3 %collective-permute-start.1 = (f32[2,512,256]{2,1,0:T(8,128)S(1)}, f32[2,512,256]{2,1,0:T(8,128)S(1)}, u32[]{:S(2)}, u32[]{:S(2)}) collective-permute-start(f32[2,512,256]{2,1,0:T(8,128)S(1)} %stack_kernel.1.near_ref), channel_id=1, source_target_pairs={{0,1},{1,0},{2,3},{3,2},{4,5},{5,4},{6,7},{7,6},{8,9},{9,8},{10,11... | collective-permute-start | bytes 3145736 | tf_op jit(solution)/shard_map/ppermute | solution.py:149
  27.2 2.3 %collective-permute-done.1.cores_ref = f32[2,512,256]{2,1,0:T(8,128)S(1)} collective-permute-done((f32[2,512,256]{2,1,0:T(8,128)S(1)}, f32[2,512,256]{2,1,0:T(8,128)S(1)}, u32[]{:S(2)}, u32[]{:S(2)}) %collective-permute-start.1) | collective-permute-done | bytes 1048608 | tf_op jit(solution)/shard_map/ppermute | solution.py:149
  29.5 0.8 self_kernel.1.self_ref
  30.3 5.8 %all-to-all-done.1.mate_ref = f32[32,2,8,256]{3,2,1,0:T(8,128)S(1)} async-done(((f32[32,2,8,256]{3,2,1,0:T(8,128)}), f32[32,2,8,256]{3,2,1,0:T(8,128)S(1)}, u32[]{:S(2)}, u32[]{:S(2)}) %all-to-all-start.1) | async-done | bytes 524320 | tf_op jit(solution)/shard_map/all_to_all | solution.py:147
  36.1 1.4 %cross_kernel.1 = f32[4,4,2,8,512]{4,3,2,1,0:T(8,128)S(1)} custom-call(s32[8,2]{1,0:T(8,128)S(1)} %copy.5.partner_ref, f32[2,512,256]{2,1,0:T(8,128)S(1)} %stack_kernel.1.near_ref, f32[2,512,256]{2,1,0:T(8,128)S(1)} %collective-permute-done.1.cores_ref, f32[32,2,8,256]{3,2,1,0:T(8,128)S(1)} %all-to-all-done.1.mate_ref, f32[128,512]{1,0:T(8,128)S(1)} %self_kernel.1.self_ref), custom_call_target="tpu_custom_call" | custom-call | tf_op jit(solution)/shard_map/cross_kernel/pallas_call | solution.py:31
  37.5 21.4 %all_to_all.20.terms_ref = f32[4,4,2,8,512]{4,3,2,1,0:T(8,128)S(1)} all-to-all(f32[4,4,2,8,512]{4,3,2,1,0:T(8,128)S(1)} %cross_kernel.1), channel_id=1, replica_groups=mesh['grp'=8,'zo'=4,'zm'=2,'zl'=2,'xh'=2,'core'=2] {'zm','xh'}, dimensions={0} | all-to-all | bytes 1048576 | tf_op jit(solution)/shard_map/all_to_all | solution.py:161
  59.0 24.3 %all_to_all.21.terms_ref = f32[4,2,8,512]{3,2,1,0:T(8,128)S(1)} all-to-all(f32[4,2,8,512]{3,2,1,0:T(8,128)S(1)} %middle_kernel.1), channel_id=1, replica_groups=mesh['grp'=8,'zo'=4,'zm'=2,'zl'=2,'xh'=2,'core'=2] {'zo'}, dimensions={0} | all-to-all | bytes 262144 | tf_op jit(solution)/shard_map/all_to_all | solution.py:163
  83.2 0.6 total_kernel.1
  (1 shorter events, 0.0 us)
Async XLA Ops:
  0.6 6.1 %copy-start = (f32[1,512,256]{2,1,0:T(8,128)S(1)}, f32[1,512,256]{2,1,0:T(8,128)}, u32[]{:S(2)}) copy-start(f32[1,512,256]{2,1,0:T(8,128)} %param.2) | copy-start | bytes 1572868
  0.6 13.6 %all-to-all-start = ((f32[8,64,256]{2,1,0:T(8,128)}), f32[8,64,256]{2,1,0:T(8,128)S(1)}, u32[]{:S(2)}, u32[]{:S(2)}) async-start(f32[8,64,256]{2,1,0:T(8,128)} %bitcast.2), calls=%async_computation | async-start | bytes 1048576 | tf_op jit(solution)/shard_map/all_to_all | solution.py:144
  6.7 3.6 %copy-start.1 = (s32[8,2]{0,1:T(2,128)S(1)}, s32[8,2]{0,1:T(2,128)}, u32[]{:S(2)}) copy-start(s32[8,2]{0,1:T(2,128)} %param.3) | copy-start | bytes 196
  6.7 18.1 %collective-permute-start = (f32[512,256]{1,0:T(8,128)S(1)}, f32[512,256]{1,0:T(8,128)S(1)}, u32[]{:S(2)}, u32[]{:S(2)}) collective-permute-start(f32[512,256]{1,0:T(8,128)S(1)} %bitcast.3), channel_id=1, source_target_pairs={{0,4},{4,0},{1,5},{5,1},{2,6},{6,2},{3,7},{7,3},{8,12},{12,8},{9,1... | collective-permute-start | bytes 1572872 | tf_op jit(solution)/shard_map/ppermute | solution.py:145
  15.8 20.3 %all-to-all-start.1 = ((f32[32,2,8,256]{3,2,1,0:T(8,128)}), f32[32,2,8,256]{3,2,1,0:T(8,128)S(1)}, u32[]{:S(2)}, u32[]{:S(2)}) async-start(f32[32,2,8,256]{3,2,1,0:T(8,128)} %route_kernel.1), calls=%async_computation.1 | async-start | bytes 1048576 | tf_op jit(solution)/shard_map/all_to_all | solution.py:147
  24.9 4.6 %collective-permute-start.1 = (f32[2,512,256]{2,1,0:T(8,128)S(1)}, f32[2,512,256]{2,1,0:T(8,128)S(1)}, u32[]{:S(2)}, u32[]{:S(2)}) collective-permute-start(f32[2,512,256]{2,1,0:T(8,128)S(1)} %stack_kernel.1.near_ref), channel_id=1, source_target_pairs={{0,1},{1,0},{2,3},{3,2},{4,5},{5,4},{6,7},{7,6},{8,9},{9,8},{10,11... | collective-permute-start | bytes 3145736 | tf_op jit(solution)/shard_map/ppermute | solution.py:149

commit v3 on v2

--- a/solution.py
+++ b/solution.py
@@ -89,20 +89,31 @@
     return lax.axis_index("zl") * 2 + lax.axis_index("core")
 
 
-def self_kernel(near_ref, cores_ref, out_ref, rows_ref):
+def self_kernel(near_ref, cores_ref, keep_ref, send_ref, rows_ref):
     me = member()
+    xh = lax.axis_index("xh")
     blocks = blocks_of(near_ref, cores_ref)
 
     def fill(i):
-        for band in range(BANDS):
-            for xh in range(2):
-                start = pl.multiple_of(band * BAND + run_of(me, xh) * RUN, RUN)
-                rows_ref[pl.ds((band * 2 + xh) * RUN, RUN), :] = blocks[i][pl.ds(start, RUN), :]
+        for part in range(2):
+            for band in range(BANDS):
+                start = pl.multiple_of(band * BAND + run_of(me, xh ^ part) * RUN, RUN)
+                rows_ref[pl.ds((part * BANDS + band) * RUN, RUN), :] = blocks[i][pl.ds(start, RUN), :]
 
-    out_ref[...] = products(blocks, rows_ref, fill)
+    result = products(blocks, rows_ref, fill)
+    for band in range(BANDS):
+        keep_ref[band] = result[band * RUN : (band + 1) * RUN]
+        send_ref[band] = result[(BANDS + band) * RUN : (BANDS + band + 1) * RUN]
 
 
-def cross_kernel(partner_ref, near_ref, cores_ref, mate_ref, self_ref, out_ref, rows_ref):
+def half_kernel(kept_ref, got_ref, keep_ref, send_ref):
+    zm = lax.axis_index("zm")
+    for zo in range(4):
+        keep_ref[zo] = kept_ref[zo * 2 + zm] + got_ref[zo * 2 + zm]
+        send_ref[zo] = kept_ref[zo * 2 + 1 - zm] + got_ref[zo * 2 + 1 - zm]
+
+
+def cross_kernel(partner_ref, near_ref, cores_ref, mate_ref, out_ref, rows_ref):
     me = member()
     offset = partner_ref[lax.axis_index("grp"), 1]
     shift = offset // BAND
@@ -122,12 +133,13 @@
     for band in range(BANDS):
         for xh in range(2):
             at = (band * 2 + xh) * RUN
-            out_ref[band % 2 * 2 + xh, band // 2, 0] = self_ref[at : at + RUN]
-            out_ref[band % 2 * 2 + xh, band // 2, 1] = cross[at : at + RUN]
+            out_ref[band % 2 * 2 + xh, band // 2] = cross[at : at + RUN]
 
 
-def middle_kernel(terms_ref, out_ref):
-    out_ref[...] = terms_ref[0] + terms_ref[1] + terms_ref[2] + terms_ref[3]
+def middle_kernel(kept_ref, got_ref, cross_ref, out_ref):
+    for zo in range(4):
+        out_ref[zo, 0] = kept_ref[zo] + got_ref[zo]
+        out_ref[zo, 1] = cross_ref[0, zo] + cross_ref[1, zo] + cross_ref[2, zo] + cross_ref[3, zo]
 
 
 def total_kernel(terms_ref, self_ref, cross_ref):
@@ -148,18 +160,15 @@
     near = call(stack_kernel, (2, ROWS, FEATS), [VMEM, VMEM], (own, above), 8)
     cores = lax.ppermute(near, "core", SWAP)
     scratch = [pltpu.VMEM((MINE, FEATS), jnp.float32)]
-    self_rows = call(self_kernel, (MINE, ROWS), [VMEM, VMEM], (near, cores), 12, HINT, scratch)
-    terms = call(
-        cross_kernel,
-        (4, 4, 2, RUN, ROWS),
-        [SMEM] + [VMEM] * 4,
-        (partner, near, cores, mate, self_rows),
-        12,
-        0,
-        scratch,
+    bands, some = (BANDS, RUN, ROWS), (4, RUN, ROWS)
+    kept, sent = call(self_kernel, [bands] * 2, [VMEM, VMEM], (near, cores), 12, HINT, scratch)
+    kept, sent = call(half_kernel, [some] * 2, [VMEM, VMEM], (kept, lax.ppermute(sent, "xh", SWAP)), 8, 2 * HINT)
+    got = lax.ppermute(sent, "zm", SWAP)
+    cross = call(
+        cross_kernel, (4, 4, RUN, ROWS), [SMEM] + [VMEM] * 3, (partner, near, cores, mate), 12, 0, scratch
     )
-    terms = lax.all_to_all(terms, ("zm", "xh"), 0, 0)
-    terms = call(middle_kernel, (4, 2, RUN, ROWS), [VMEM], (terms,), 8)
+    cross = lax.all_to_all(cross, ("zm", "xh"), 0, 0)
+    terms = call(middle_kernel, (4, 2, RUN, ROWS), [VMEM] * 3, (kept, got, cross), 8)
     terms = lax.all_to_all(terms, "zo", 0, 0)
     return tuple(call(total_kernel, [(1, RUN, ROWS)] * 2, [VMEM], (terms,), 8))
 

time: 84.2 us -> 81.5 us (0.968)
  the two profiles are of different devices: /device:TPU:1 before, /device:TPU:4 now
where the time goes in v3:
time: 81.5 us; the launch traced here: 81 us
  starting transfers between devices  31.6 us (39%)
  blocking collectives  26.1 us (32%)
  waiting for transfers between devices  17.3 us (21%)
  Pallas kernels  5.19 us (6%)
    all_to_all x1, blocking collectives, local(): terms = lax.all_to_all(terms, 'zo', 0, 0)  26.1 us
    ppermute x1, waiting for transfers between devices, local(): got = lax.ppermute(sent, 'zm', SWAP)  7.86 us
    all_to_all x1, starting transfers between devices, local(): cross = lax.all_to_all(cross, ('zm', 'xh'), 0, 0)  7.49 us
    all_to_all x1, waiting for transfers between devices, local(): chunks = lax.all_to_all(own.reshape(GROUPS, BAND, FEATS), 'grp', 0, 0)  6.14 us
    all_to_all x1, starting transfers between devices, local(): chunks = lax.all_to_all(own.reshape(GROUPS, BAND, FEATS), 'grp', 0, 0)  5.25 us
    pallas_call x7, Pallas kernels, call(): pl.pallas_call(kernel, out_shape=[one(dims) for dims in shape] if several...  5.19 us
    all_to_all x1, starting transfers between devices, local(): mate = lax.all_to_all(routed, ('grp', 'zl', 'core'), 0, 0)  4.48 us
    ppermute x1, starting transfers between devices, local(): got = lax.ppermute(sent, 'zm', SWAP)  4.27 us
  transfers between devices with their start and end apart: 7, of which 4 were waited for; matrix products, arithmetic and copies ran while one was open for 0% of the time, Pallas kernels for 6%

profile of v3, /device:TPU:4, one launch (start us, length us, event | category | flops | bytes accessed | tf_op | source)
XLA Modules:
  0.0 81.0 jit_solution(11890550115425264929)
XLA Ops:
  0.6 0.0 copy-start
  0.6 5.2 %all-to-all-start = ((f32[8,64,256]{2,1,0:T(8,128)}), f32[8,64,256]{2,1,0:T(8,128)S(1)}, u32[]{:S(2)}, u32[]{:S(2)}) async-start(f32[8,64,256]{2,1,0:T(8,128)} %bitcast.2), calls=%async_computation | async-start | bytes 1048576 | tf_op jit(solution)/shard_map/all_to_all | solution.py:156
  5.9 0.0 copy-start.1
  5.9 0.0 copy-done
  5.9 3.8 %collective-permute-start = (f32[512,256]{1,0:T(8,128)S(1)}, f32[512,256]{1,0:T(8,128)S(1)}, u32[]{:S(2)}, u32[]{:S(2)}) collective-permute-start(f32[512,256]{1,0:T(8,128)S(1)} %bitcast.3), channel_id=1, source_target_pairs={{0,4},{4,0},{1,5},{5,1},{2,6},{6,2},{3,7},{7,3},{8,12},{12,8},{9,1... | collective-permute-start | bytes 1572872 | tf_op jit(solution)/shard_map/ppermute | solution.py:157
  9.7 0.0 copy-done.1
  9.7 0.1 copy.5.partner_ref
  9.8 6.1 %all-to-all-done.rows_ref = f32[8,64,256]{2,1,0:T(8,128)S(1)} async-done(((f32[8,64,256]{2,1,0:T(8,128)}), f32[8,64,256]{2,1,0:T(8,128)S(1)}, u32[]{:S(2)}, u32[]{:S(2)}) %all-to-all-start) | async-done | bytes 524320 | tf_op jit(solution)/shard_map/all_to_all | solution.py:156
  16.0 1.5 %route_kernel.1 = f32[32,2,8,256]{3,2,1,0:T(8,128)} custom-call(s32[8,2]{1,0:T(8,128)S(1)} %copy.5.partner_ref, f32[8,64,256]{2,1,0:T(8,128)S(1)} %all-to-all-done.rows_ref), custom_call_target="tpu_custom_call" | custom-call | tf_op jit(solution)/shard_map/route_kernel/pallas_call | solution.py:31
  17.5 4.5 %all-to-all-start.1 = ((f32[32,2,8,256]{3,2,1,0:T(8,128)}), f32[32,2,8,256]{3,2,1,0:T(8,128)S(1)}, u32[]{:S(2)}, u32[]{:S(2)}) async-start(f32[32,2,8,256]{3,2,1,0:T(8,128)} %route_kernel.1), calls=%async_computation.1 | async-start | bytes 1048576 | tf_op jit(solution)/shard_map/all_to_all | solution.py:159
  22.0 0.0 collective-permute-done.above_ref
  22.0 0.1 stack_kernel.1.near_ref
  22.0 2.2 %collective-permute-start.1 = (f32[2,512,256]{2,1,0:T(8,128)S(1)}, f32[2,512,256]{2,1,0:T(8,128)S(1)}, u32[]{:S(2)}, u32[]{:S(2)}) collective-permute-start(f32[2,512,256]{2,1,0:T(8,128)S(1)} %stack_kernel.1.near_ref), channel_id=1, source_target_pairs={{0,1},{1,0},{2,3},{3,2},{4,5},{5,4},{6,7},{7,6},{8,9},{9,8},{10,11... | collective-permute-start | bytes 3145736 | tf_op jit(solution)/shard_map/ppermute | solution.py:161
  24.2 2.4 %collective-permute-done.1.cores_ref = f32[2,512,256]{2,1,0:T(8,128)S(1)} collective-permute-done((f32[2,512,256]{2,1,0:T(8,128)S(1)}, f32[2,512,256]{2,1,0:T(8,128)S(1)}, u32[]{:S(2)}, u32[]{:S(2)}) %collective-permute-start.1) | collective-permute-done | bytes 1048608 | tf_op jit(solution)/shard_map/ppermute | solution.py:161
  26.6 0.8 %self_kernel.1 = (f32[8,8,512]{2,1,0:T(8,128)S(1)}, f32[8,8,512]{2,1,0:T(8,128)S(1)}) custom-call(f32[2,512,256]{2,1,0:T(8,128)S(1)} %stack_kernel.1.near_ref, f32[2,512,256]{2,1,0:T(8,128)S(1)} %collective-permute-done.1.cores_ref), custom_call_target="tpu_custom_call" | custom-call | flops 5000000000 | tf_op jit(solution)/shard_map/self_kernel/pallas_call | solution.py:31
  27.4 4.1 %collective-permute-start.2 = (f32[8,8,512]{2,1,0:T(8,128)S(1)}, f32[8,8,512]{2,1,0:T(8,128)S(1)}, u32[]{:S(2)}, u32[]{:S(2)}) collective-permute-start(f32[8,8,512]{2,1,0:T(8,128)S(1)} %get-tuple-element.7), channel_id=1, source_target_pairs={{0,2},{2,0},{1,3},{3,1},{4,6},{6,4},{5,7},{7,5},{8,10},{10,8},{9,1... | collective-permute-start | bytes 393224 | tf_op jit(solution)/shard_map/ppermute | solution.py:165
  31.6 0.9 %all-to-all-done.1.mate_ref = f32[32,2,8,256]{3,2,1,0:T(8,128)S(1)} async-done(((f32[32,2,8,256]{3,2,1,0:T(8,128)}), f32[32,2,8,256]{3,2,1,0:T(8,128)S(1)}, u32[]{:S(2)}, u32[]{:S(2)}) %all-to-all-start.1) | async-done | bytes 524320 | tf_op jit(solution)/shard_map/all_to_all | solution.py:159
  32.5 2.1 %cross_kernel.1 = f32[4,4,8,512]{3,2,1,0:T(8,128)} custom-call(s32[8,2]{1,0:T(8,128)S(1)} %copy.5.partner_ref, f32[2,512,256]{2,1,0:T(8,128)S(1)} %stack_kernel.1.near_ref, f32[2,512,256]{2,1,0:T(8,128)S(1)} %collective-permute-done.1.cores_ref, f32[32,2,8,256]{3,2,1,0:T(8,128)S(1)} %all-to-all-done.1.mate_ref), custom_call_target="tpu_custom_call" | custom-call | tf_op jit(solution)/shard_map/cross_kernel/pallas_call | solution.py:31
  34.7 7.5 %all-to-all-start.2 = ((f32[4,4,8,512]{3,2,1,0:T(8,128)}), f32[4,4,8,512]{3,2,1,0:T(8,128)S(1)}, u32[]{:S(2)}, u32[]{:S(2)}) async-start(f32[4,4,8,512]{3,2,1,0:T(8,128)} %cross_kernel.1), calls=%async_computation.2 | async-start | bytes 524288 | tf_op jit(solution)/shard_map/all_to_all | solution.py:170
  42.1 0.0 collective-permute-done.2.got_ref
  42.2 4.3 %collective-permute-start.3 = (f32[4,8,512]{2,1,0:T(8,128)S(1)}, f32[4,8,512]{2,1,0:T(8,128)S(1)}, u32[]{:S(2)}, u32[]{:S(2)}) collective-permute-start(f32[4,8,512]{2,1,0:T(8,128)S(1)} %get-tuple-element.9), channel_id=1, source_target_pairs={{0,8},{8,0},{1,9},{9,1},{2,10},{10,2},{3,11},{11,3},{4,12},{12,4},... | collective-permute-start | bytes 196616 | tf_op jit(solution)/shard_map/ppermute | solution.py:166
  46.4 7.9 %collective-permute-done.3.got_ref = f32[4,8,512]{2,1,0:T(8,128)S(1)} collective-permute-done((f32[4,8,512]{2,1,0:T(8,128)S(1)}, f32[4,8,512]{2,1,0:T(8,128)S(1)}, u32[]{:S(2)}, u32[]{:S(2)}) %collective-permute-start.3) | collective-permute-done | bytes 65568 | tf_op jit(solution)/shard_map/ppermute | solution.py:166
  54.3 0.0 all-to-all-done.2.cross_ref
  54.3 26.1 %all_to_all.20.terms_ref = f32[4,2,8,512]{3,2,1,0:T(8,128)S(1)} all-to-all(f32[4,2,8,512]{3,2,1,0:T(8,128)S(1)} %middle_kernel.1), channel_id=1, replica_groups=mesh['grp'=8,'zo'=4,'zm'=2,'zl'=2,'xh'=2,'core'=2] {'zo'}, dimensions={0} | all-to-all | bytes 262144 | tf_op jit(solution)/shard_map/all_to_all | solution.py:172
  80.4 0.6 total_kernel.1
  (2 shorter events, 0.0 us)
Async XLA Ops:
  0.6 5.3 %copy-start = (f32[1,512,256]{2,1,0:T(8,128)S(1)}, f32[1,512,256]{2,1,0:T(8,128)}, u32[]{:S(2)}) copy-start(f32[1,512,256]{2,1,0:T(8,128)} %param.2) | copy-start | bytes 1572868
  0.6 15.3 %all-to-all-start = ((f32[8,64,256]{2,1,0:T(8,128)}), f32[8,64,256]{2,1,0:T(8,128)S(1)}, u32[]{:S(2)}, u32[]{:S(2)}) async-start(f32[8,64,256]{2,1,0:T(8,128)} %bitcast.2), calls=%async_computation | async-start | bytes 1048576 | tf_op jit(solution)/shard_map/all_to_all | solution.py:156
  5.9 3.9 %copy-start.1 = (s32[8,2]{0,1:T(2,128)S(1)}, s32[8,2]{0,1:T(2,128)}, u32[]{:S(2)}) copy-start(s32[8,2]{0,1:T(2,128)} %param.3) | copy-start | bytes 196
  5.9 16.1 %collective-permute-start = (f32[512,256]{1,0:T(8,128)S(1)}, f32[512,256]{1,0:T(8,128)S(1)}, u32[]{:S(2)}, u32[]{:S(2)}) collective-permute-start(f32[512,256]{1,0:T(8,128)S(1)} %bitcast.3), channel_id=1, source_target_pairs={{0,4},{4,0},{1,5},{5,1},{2,6},{6,2},{3,7},{7,3},{8,12},{12,8},{9,1... | collective-permute-start | bytes 1572872 | tf_op jit(solution)/shard_map/ppermute | solution.py:157
  17.5 15.0 %all-to-all-start.1 = ((f32[32,2,8,256]{3,2,1,0:T(8,128)}), f32[32,2,8,256]{3,2,1,0:T(8,128)S(1)}, u32[]{:S(2)}, u32[]{:S(2)}) async-start(f32[32,2,8,256]{3,2,1,0:T(8,128)} %route_kernel.1), calls=%async_computation.1 | async-start | bytes 1048576 | tf_op jit(solution)/shard_map/all_to_all | solution.py:159
  22.0 4.6 %collective-permute-start.1 = (f32[2,512,256]{2,1,0:T(8,128)S(1)}, f32[2,512,256]{2,1,0:T(8,128)S(1)}, u32[]{:S(2)}, u32[]{:S(2)}) collective-permute-start(f32[2,512,256]{2,1,0:T(8,128)S(1)} %stack_kernel.1.near_ref), channel_id=1, source_target_pairs={{0,1},{1,0},{2,3},{3,2},{4,5},{5,4},{6,7},{7,6},{8,9},{9,8},{10,11... | collective-permute-start | bytes 3145736 | tf_op jit(solution)/shard_map/ppermute | solution.py:161
  27.4 14.7 %collective-permute-start.2 = (f32[8,8,512]{2,1,0:T(8,128)S(1)}, f32[8,8,512]{2,1,0:T(8,128)S(1)}, u32[]{:S(2)}, u32[]{:S(2)}) collective-permute-start(f32[8,8,512]{2,1,0:T(8,128)S(1)} %get-tuple-element.7), channel_id=1, source_target_pairs={{0,2},{2,0},{1,3},{3,1},{4,6},{6,4},{5,7},{7,5},{8,10},{10,8},{9,1... | collective-permute-start | bytes 393224 | tf_op jit(solution)/shard_map/ppermute | solution.py:165
  34.7 19.7 %all-to-all-start.2 = ((f32[4,4,8,512]{3,2,1,0:T(8,128)}), f32[4,4,8,512]{3,2,1,0:T(8,128)S(1)}, u32[]{:S(2)}, u32[]{:S(2)}) async-start(f32[4,4,8,512]{3,2,1,0:T(8,128)} %cross_kernel.1), calls=%async_computation.2 | async-start | bytes 524288 | tf_op jit(solution)/shard_map/all_to_all | solution.py:170
  42.2 12.1 %collective-permute-start.3 = (f32[4,8,512]{2,1,0:T(8,128)S(1)}, f32[4,8,512]{2,1,0:T(8,128)S(1)}, u32[]{:S(2)}, u32[]{:S(2)}) collective-permute-start(f32[4,8,512]{2,1,0:T(8,128)S(1)} %get-tuple-element.9), channel_id=1, source_target_pairs={{0,8},{8,0},{1,9},{9,1},{2,10},{10,2},{3,11},{11,3},{4,12},{12,4},... | collective-permute-start | bytes 196616 | tf_op jit(solution)/shard_map/ppermute | solution.py:166

commit v4 on v3

--- a/solution.py
+++ b/solution.py
@@ -19,6 +19,7 @@
 SWAP = [(0, 1), (1, 0)]
 NEAR = (0, 2, 1, 3)
 HINT = 5_000_000_000
+QUARTERS = (2, 3, 0, 1)
 VMEM = pl.BlockSpec(memory_space=pltpu.VMEM)
 SMEM = pl.BlockSpec(memory_space=pltpu.SMEM)
 
@@ -91,14 +92,15 @@
 
 def self_kernel(near_ref, cores_ref, keep_ref, send_ref, rows_ref):
     me = member()
-    xh = lax.axis_index("xh")
+    zm = lax.axis_index("zm")
     blocks = blocks_of(near_ref, cores_ref)
 
     def fill(i):
         for part in range(2):
-            for band in range(BANDS):
-                start = pl.multiple_of(band * BAND + run_of(me, xh ^ part) * RUN, RUN)
-                rows_ref[pl.ds((part * BANDS + band) * RUN, RUN), :] = blocks[i][pl.ds(start, RUN), :]
+            for at in range(BANDS):
+                band = at // 2 * 2 + (zm ^ part)
+                start = pl.multiple_of(band * BAND + run_of(me, at % 2) * RUN, RUN)
+                rows_ref[pl.ds((part * BANDS + at) * RUN, RUN), :] = blocks[i][pl.ds(start, RUN), :]
 
     result = products(blocks, rows_ref, fill)
     for band in range(BANDS):
@@ -107,10 +109,10 @@
 
 
 def half_kernel(kept_ref, got_ref, keep_ref, send_ref):
-    zm = lax.axis_index("zm")
+    xh = lax.axis_index("xh")
     for zo in range(4):
-        keep_ref[zo] = kept_ref[zo * 2 + zm] + got_ref[zo * 2 + zm]
-        send_ref[zo] = kept_ref[zo * 2 + 1 - zm] + got_ref[zo * 2 + 1 - zm]
+        keep_ref[zo] = kept_ref[zo * 2 + xh] + got_ref[zo * 2 + xh]
+        send_ref[zo] = kept_ref[zo * 2 + 1 - xh] + got_ref[zo * 2 + 1 - xh]
 
 
 def cross_kernel(partner_ref, near_ref, cores_ref, mate_ref, out_ref, rows_ref):
@@ -137,9 +139,9 @@
 
 
 def middle_kernel(kept_ref, got_ref, cross_ref, out_ref):
-    for zo in range(4):
-        out_ref[zo, 0] = kept_ref[zo] + got_ref[zo]
-        out_ref[zo, 1] = cross_ref[0, zo] + cross_ref[1, zo] + cross_ref[2, zo] + cross_ref[3, zo]
+    for at, zo in enumerate(QUARTERS):
+        out_ref[at, 0] = kept_ref[zo] + got_ref[zo]
+        out_ref[at, 1] = cross_ref[0, zo] + cross_ref[1, zo] + cross_ref[2, zo] + cross_ref[3, zo]
 
 
 def total_kernel(terms_ref, self_ref, cross_ref):
@@ -162,14 +164,14 @@
     scratch = [pltpu.VMEM((MINE, FEATS), jnp.float32)]
     bands, some = (BANDS, RUN, ROWS), (4, RUN, ROWS)
     kept, sent = call(self_kernel, [bands] * 2, [VMEM, VMEM], (near, cores), 12, HINT, scratch)
-    kept, sent = call(half_kernel, [some] * 2, [VMEM, VMEM], (kept, lax.ppermute(sent, "xh", SWAP)), 8, 2 * HINT)
-    got = lax.ppermute(sent, "zm", SWAP)
+    kept, sent = call(half_kernel, [some] * 2, [VMEM, VMEM], (kept, lax.ppermute(sent, "zm", SWAP)), 8, 2 * HINT)
+    got = lax.ppermute(sent, "xh", SWAP)
     cross = call(
         cross_kernel, (4, 4, RUN, ROWS), [SMEM] + [VMEM] * 3, (partner, near, cores, mate), 12, 0, scratch
     )
     cross = lax.all_to_all(cross, ("zm", "xh"), 0, 0)
     terms = call(middle_kernel, (4, 2, RUN, ROWS), [VMEM] * 3, (kept, got, cross), 8)
-    terms = lax.all_to_all(terms, "zo", 0, 0)
+    terms = lax.all_to_all(terms, "zo", 0, 0, axis_index_groups=[list(QUARTERS)])
     return tuple(call(total_kernel, [(1, RUN, ROWS)] * 2, [VMEM], (terms,), 8))
 
 

time: 81.5 us -> 73 us (0.90)
  the two profiles are of different devices: /device:TPU:4 before, /device:TPU:1 now
where the time goes in v4:
time: 73 us; the launch traced here: 72.5 us
  starting transfers between devices  34.4 us (47%)
  blocking collectives  18.3 us (25%)
  waiting for transfers between devices  13.8 us (19%)
  Pallas kernels  5.2 us (7%)
    all_to_all x1, blocking collectives, local(): lax.all_to_all(terms, 'zo', 0, 0, axis_index_groups=[list(QUARTERS)])  18.3 us
    all_to_all x1, starting transfers between devices, local(): mate = lax.all_to_all(routed, ('grp', 'zl', 'core'), 0, 0)  9.06 us
    all_to_all x1, starting transfers between devices, local(): chunks = lax.all_to_all(own.reshape(GROUPS, BAND, FEATS), 'grp', 0, 0)  6.09 us
    pallas_call x7, Pallas kernels, call(): pl.pallas_call(kernel, out_shape=[one(dims) for dims in shape] if several...  5.2 us
    all_to_all x1, starting transfers between devices, local(): cross = lax.all_to_all(cross, ('zm', 'xh'), 0, 0)  5 us
    ppermute x1, starting transfers between devices, local(): got = lax.ppermute(sent, 'xh', SWAP)  4.88 us
    all_to_all x1, waiting for transfers between devices, local(): chunks = lax.all_to_all(own.reshape(GROUPS, BAND, FEATS), 'grp', 0, 0)  3.88 us
    ppermute x1, starting transfers between devices, local(): lax.ppermute(sent, 'zm', SWAP)  3.58 us
  transfers between devices with their start and end apart: 7, of which 5 were waited for; matrix products, arithmetic and copies ran while one was open for 0% of the time, Pallas kernels for 6%

profile of v4, /device:TPU:1, one launch (start us, length us, event | category | flops | bytes accessed | tf_op | source)
XLA Modules:
  0.0 72.5 jit_solution(8235292712357812373)
XLA Ops:
  0.6 0.0 copy-start
  0.6 6.1 %all-to-all-start = ((f32[8,64,256]{2,1,0:T(8,128)}), f32[8,64,256]{2,1,0:T(8,128)S(1)}, u32[]{:S(2)}, u32[]{:S(2)}) async-start(f32[8,64,256]{2,1,0:T(8,128)} %bitcast.2), calls=%async_computation | async-start | bytes 1048576 | tf_op jit(solution)/shard_map/all_to_all | solution.py:158
  6.7 0.0 copy-start.1
  6.7 0.0 copy-done
  6.7 3.5 %collective-permute-start = (f32[512,256]{1,0:T(8,128)S(1)}, f32[512,256]{1,0:T(8,128)S(1)}, u32[]{:S(2)}, u32[]{:S(2)}) collective-permute-start(f32[512,256]{1,0:T(8,128)S(1)} %bitcast.3), channel_id=1, source_target_pairs={{0,4},{4,0},{1,5},{5,1},{2,6},{6,2},{3,7},{7,3},{8,12},{12,8},{9,1... | collective-permute-start | bytes 1572872 | tf_op jit(solution)/shard_map/ppermute | solution.py:159
  10.3 0.0 copy-done.1
  10.3 0.1 copy.5.partner_ref
  10.4 3.9 %all-to-all-done.rows_ref = f32[8,64,256]{2,1,0:T(8,128)S(1)} async-done(((f32[8,64,256]{2,1,0:T(8,128)}), f32[8,64,256]{2,1,0:T(8,128)S(1)}, u32[]{:S(2)}, u32[]{:S(2)}) %all-to-all-start) | async-done | bytes 524320 | tf_op jit(solution)/shard_map/all_to_all | solution.py:158
  14.3 1.5 %route_kernel.1 = f32[32,2,8,256]{3,2,1,0:T(8,128)} custom-call(s32[8,2]{1,0:T(8,128)S(1)} %copy.5.partner_ref, f32[8,64,256]{2,1,0:T(8,128)S(1)} %all-to-all-done.rows_ref), custom_call_target="tpu_custom_call" | custom-call | tf_op jit(solution)/shard_map/route_kernel/pallas_call | solution.py:32
  15.8 9.1 %all-to-all-start.1 = ((f32[32,2,8,256]{3,2,1,0:T(8,128)}), f32[32,2,8,256]{3,2,1,0:T(8,128)S(1)}, u32[]{:S(2)}, u32[]{:S(2)}) async-start(f32[32,2,8,256]{3,2,1,0:T(8,128)} %route_kernel.1), calls=%async_computation.1 | async-start | bytes 1048576 | tf_op jit(solution)/shard_map/all_to_all | solution.py:161
  24.8 0.0 collective-permute-done.above_ref
  24.8 0.1 stack_kernel.1.near_ref
  24.9 2.3 %collective-permute-start.1 = (f32[2,512,256]{2,1,0:T(8,128)S(1)}, f32[2,512,256]{2,1,0:T(8,128)S(1)}, u32[]{:S(2)}, u32[]{:S(2)}) collective-permute-start(f32[2,512,256]{2,1,0:T(8,128)S(1)} %stack_kernel.1.near_ref), channel_id=1, source_target_pairs={{0,1},{1,0},{2,3},{3,2},{4,5},{5,4},{6,7},{7,6},{8,9},{9,8},{10,11... | collective-permute-start | bytes 3145736 | tf_op jit(solution)/shard_map/ppermute | solution.py:163
  27.2 2.3 %collective-permute-done.1.cores_ref = f32[2,512,256]{2,1,0:T(8,128)S(1)} collective-permute-done((f32[2,512,256]{2,1,0:T(8,128)S(1)}, f32[2,512,256]{2,1,0:T(8,128)S(1)}, u32[]{:S(2)}, u32[]{:S(2)}) %collective-permute-start.1) | collective-permute-done | bytes 1048608 | tf_op jit(solution)/shard_map/ppermute | solution.py:163
  29.5 0.8 %self_kernel.1 = (f32[8,8,512]{2,1,0:T(8,128)S(1)}, f32[8,8,512]{2,1,0:T(8,128)S(1)}) custom-call(f32[2,512,256]{2,1,0:T(8,128)S(1)} %stack_kernel.1.near_ref, f32[2,512,256]{2,1,0:T(8,128)S(1)} %collective-permute-done.1.cores_ref), custom_call_target="tpu_custom_call" | custom-call | flops 5000000000 | tf_op jit(solution)/shard_map/self_kernel/pallas_call | solution.py:32
  30.3 3.6 %collective-permute-start.2 = (f32[8,8,512]{2,1,0:T(8,128)S(1)}, f32[8,8,512]{2,1,0:T(8,128)S(1)}, u32[]{:S(2)}, u32[]{:S(2)}) collective-permute-start(f32[8,8,512]{2,1,0:T(8,128)S(1)} %get-tuple-element.7), channel_id=1, source_target_pairs={{0,8},{8,0},{1,9},{9,1},{2,10},{10,2},{3,11},{11,3},{4,12},{12,4},... | collective-permute-start | bytes 393224 | tf_op jit(solution)/shard_map/ppermute | solution.py:167
  33.9 2.2 %all-to-all-done.1.mate_ref = f32[32,2,8,256]{3,2,1,0:T(8,128)S(1)} async-done(((f32[32,2,8,256]{3,2,1,0:T(8,128)}), f32[32,2,8,256]{3,2,1,0:T(8,128)S(1)}, u32[]{:S(2)}, u32[]{:S(2)}) %all-to-all-start.1) | async-done | bytes 524320 | tf_op jit(solution)/shard_map/all_to_all | solution.py:161
  36.1 2.1 %cross_kernel.1 = f32[4,4,8,512]{3,2,1,0:T(8,128)} custom-call(s32[8,2]{1,0:T(8,128)S(1)} %copy.5.partner_ref, f32[2,512,256]{2,1,0:T(8,128)S(1)} %stack_kernel.1.near_ref, f32[2,512,256]{2,1,0:T(8,128)S(1)} %collective-permute-done.1.cores_ref, f32[32,2,8,256]{3,2,1,0:T(8,128)S(1)} %all-to-all-done.1.mate_ref), custom_call_target="tpu_custom_call" | custom-call | tf_op jit(solution)/shard_map/cross_kernel/pallas_call | solution.py:32
  38.2 5.0 %all-to-all-start.2 = ((f32[4,4,8,512]{3,2,1,0:T(8,128)}), f32[4,4,8,512]{3,2,1,0:T(8,128)S(1)}, u32[]{:S(2)}, u32[]{:S(2)}) async-start(f32[4,4,8,512]{3,2,1,0:T(8,128)} %cross_kernel.1), calls=%async_computation.2 | async-start | bytes 524288 | tf_op jit(solution)/shard_map/all_to_all | solution.py:172
  43.2 0.0 collective-permute-done.2.got_ref
  43.3 4.9 %collective-permute-start.3 = (f32[4,8,512]{2,1,0:T(8,128)S(1)}, f32[4,8,512]{2,1,0:T(8,128)S(1)}, u32[]{:S(2)}, u32[]{:S(2)}) collective-permute-start(f32[4,8,512]{2,1,0:T(8,128)S(1)} %get-tuple-element.9), channel_id=1, source_target_pairs={{0,2},{2,0},{1,3},{3,1},{4,6},{6,4},{5,7},{7,5},{8,10},{10,8},{9,1... | collective-permute-start | bytes 196616 | tf_op jit(solution)/shard_map/ppermute | solution.py:168
  48.1 2.6 %collective-permute-done.3.got_ref = f32[4,8,512]{2,1,0:T(8,128)S(1)} collective-permute-done((f32[4,8,512]{2,1,0:T(8,128)S(1)}, f32[4,8,512]{2,1,0:T(8,128)S(1)}, u32[]{:S(2)}, u32[]{:S(2)}) %collective-permute-start.3) | collective-permute-done | bytes 65568 | tf_op jit(solution)/shard_map/ppermute | solution.py:168
  50.7 2.8 %all-to-all-done.2.cross_ref = f32[4,4,8,512]{3,2,1,0:T(8,128)S(1)} async-done(((f32[4,4,8,512]{3,2,1,0:T(8,128)}), f32[4,4,8,512]{3,2,1,0:T(8,128)S(1)}, u32[]{:S(2)}, u32[]{:S(2)}) %all-to-all-start.2) | async-done | bytes 262176 | tf_op jit(solution)/shard_map/all_to_all | solution.py:172
  53.5 18.3 %all_to_all.20.terms_ref = f32[4,2,8,512]{3,2,1,0:T(8,128)S(1)} all-to-all(f32[4,2,8,512]{3,2,1,0:T(8,128)S(1)} %middle_kernel.1), channel_id=1, replica_groups={{32,48,0,16},{33,49,1,17},{34,50,2,18},{35,51,3,19},{36,52,4,20},{37,53..., dimensions={0} | all-to-all | bytes 262144 | tf_op jit(solution)/shard_map/all_to_all | solution.py:174
  71.9 0.6 total_kernel.1
  (2 shorter events, 0.0 us)
Async XLA Ops:
  0.6 6.1 %copy-start = (f32[1,512,256]{2,1,0:T(8,128)S(1)}, f32[1,512,256]{2,1,0:T(8,128)}, u32[]{:S(2)}) copy-start(f32[1,512,256]{2,1,0:T(8,128)} %param.2) | copy-start | bytes 1572868
  0.6 13.6 %all-to-all-start = ((f32[8,64,256]{2,1,0:T(8,128)}), f32[8,64,256]{2,1,0:T(8,128)S(1)}, u32[]{:S(2)}, u32[]{:S(2)}) async-start(f32[8,64,256]{2,1,0:T(8,128)} %bitcast.2), calls=%async_computation | async-start | bytes 1048576 | tf_op jit(solution)/shard_map/all_to_all | solution.py:158
  6.7 3.6 %copy-start.1 = (s32[8,2]{0,1:T(2,128)S(1)}, s32[8,2]{0,1:T(2,128)}, u32[]{:S(2)}) copy-start(s32[8,2]{0,1:T(2,128)} %param.3) | copy-start | bytes 196
  6.7 18.1 %collective-permute-start = (f32[512,256]{1,0:T(8,128)S(1)}, f32[512,256]{1,0:T(8,128)S(1)}, u32[]{:S(2)}, u32[]{:S(2)}) collective-permute-start(f32[512,256]{1,0:T(8,128)S(1)} %bitcast.3), channel_id=1, source_target_pairs={{0,4},{4,0},{1,5},{5,1},{2,6},{6,2},{3,7},{7,3},{8,12},{12,8},{9,1... | collective-permute-start | bytes 1572872 | tf_op jit(solution)/shard_map/ppermute | solution.py:159
  15.8 20.3 %all-to-all-start.1 = ((f32[32,2,8,256]{3,2,1,0:T(8,128)}), f32[32,2,8,256]{3,2,1,0:T(8,128)S(1)}, u32[]{:S(2)}, u32[]{:S(2)}) async-start(f32[32,2,8,256]{3,2,1,0:T(8,128)} %route_kernel.1), calls=%async_computation.1 | async-start | bytes 1048576 | tf_op jit(solution)/shard_map/all_to_all | solution.py:161
  24.9 4.6 %collective-permute-start.1 = (f32[2,512,256]{2,1,0:T(8,128)S(1)}, f32[2,512,256]{2,1,0:T(8,128)S(1)}, u32[]{:S(2)}, u32[]{:S(2)}) collective-permute-start(f32[2,512,256]{2,1,0:T(8,128)S(1)} %stack_kernel.1.near_ref), channel_id=1, source_target_pairs={{0,1},{1,0},{2,3},{3,2},{4,5},{5,4},{6,7},{7,6},{8,9},{9,8},{10,11... | collective-permute-start | bytes 3145736 | tf_op jit(solution)/shard_map/ppermute | solution.py:163
  30.3 12.9 %collective-permute-start.2 = (f32[8,8,512]{2,1,0:T(8,128)S(1)}, f32[8,8,512]{2,1,0:T(8,128)S(1)}, u32[]{:S(2)}, u32[]{:S(2)}) collective-permute-start(f32[8,8,512]{2,1,0:T(8,128)S(1)} %get-tuple-element.7), channel_id=1, source_target_pairs={{0,8},{8,0},{1,9},{9,1},{2,10},{10,2},{3,11},{11,3},{4,12},{12,4},... | collective-permute-start | bytes 393224 | tf_op jit(solution)/shard_map/ppermute | solution.py:167
  38.2 15.3 %all-to-all-start.2 = ((f32[4,4,8,512]{3,2,1,0:T(8,128)}), f32[4,4,8,512]{3,2,1,0:T(8,128)S(1)}, u32[]{:S(2)}, u32[]{:S(2)}) async-start(f32[4,4,8,512]{3,2,1,0:T(8,128)} %cross_kernel.1), calls=%async_computation.2 | async-start | bytes 524288 | tf_op jit(solution)/shard_map/all_to_all | solution.py:172
  43.3 7.5 %collective-permute-start.3 = (f32[4,8,512]{2,1,0:T(8,128)S(1)}, f32[4,8,512]{2,1,0:T(8,128)S(1)}, u32[]{:S(2)}, u32[]{:S(2)}) collective-permute-start(f32[4,8,512]{2,1,0:T(8,128)S(1)} %get-tuple-element.9), channel_id=1, source_target_pairs={{0,2},{2,0},{1,3},{3,1},{4,6},{6,4},{5,7},{7,5},{8,10},{10,8},{9,1... | collective-permute-start | bytes 196616 | tf_op jit(solution)/shard_map/ppermute | solution.py:168

commit v5 on v4

--- a/solution.py
+++ b/solution.py
@@ -19,9 +19,13 @@
 SWAP = [(0, 1), (1, 0)]
 NEAR = (0, 2, 1, 3)
 HINT = 5_000_000_000
-QUARTERS = (2, 3, 0, 1)
+FIRST, SECOND, NARROW, WIDE = 4, 16, 1, 2
 VMEM = pl.BlockSpec(memory_space=pltpu.VMEM)
-SMEM = pl.BlockSpec(memory_space=pltpu.SMEM)
+
+
+def exchange(values, axes, first):
+    members = [i ^ first for i in range(values.shape[0])]
+    return lax.all_to_all(values, axes, 0, 0, axis_index_groups=[members])
 
 
 def call(kernel, shape, specs, arrays, limit, flops=0, scratch=()):
@@ -46,13 +50,14 @@
 
 
 def route_kernel(partner_ref, rows_ref, out_ref):
+    partner = partner_ref[...]
     for g in range(GROUPS):
-        turn = lax.rem(BAND - lax.rem(partner_ref[g, 1], BAND), BAND)
-        band = pltpu.roll(rows_ref[partner_ref[g, 0]], turn, 0)
+        turn = lax.rem(BAND - lax.rem(partner[g, 1], BAND), BAND)
+        band = pltpu.roll(rows_ref[partner[g, 0] ^ FIRST], turn, 0)
         for m in range(QUAD):
             for xh in range(2):
                 at = (m // 2 * 4 + xh * 2 + m % 2) * RUN
-                out_ref[g * QUAD + m, xh] = band[at : at + RUN]
+                out_ref[(g * QUAD + m) ^ SECOND, xh] = band[at : at + RUN]
 
 
 def stack_kernel(own_ref, above_ref, near_ref):
@@ -117,15 +122,15 @@
 
 def cross_kernel(partner_ref, near_ref, cores_ref, mate_ref, out_ref, rows_ref):
     me = member()
-    offset = partner_ref[lax.axis_index("grp"), 1]
+    offset = partner_ref[pl.ds(lax.axis_index("grp"), 1), :][0, 1]
     shift = offset // BAND
     row = lax.broadcasted_iota(jnp.int32, (RUN, FEATS), 0) + lax.rem(offset, BAND)
 
     def fill(i):
         source = me ^ NEAR[i]
         for band in range(BANDS):
-            low = lax.rem(band + shift, BANDS) * QUAD + source
-            high = lax.rem(band + shift + 1, BANDS) * QUAD + source
+            low = ((lax.rem(band + shift, BANDS) ^ FIRST) * QUAD + source) ^ SECOND
+            high = ((lax.rem(band + shift + 1, BANDS) ^ FIRST) * QUAD + source) ^ SECOND
             for xh in range(2):
                 rows_ref[pl.ds((band * 2 + xh) * RUN, RUN), :] = jnp.where(
                     row + run_of(me, xh) * RUN >= BAND, mate_ref[high, xh], mate_ref[low, xh]
@@ -135,13 +140,13 @@
     for band in range(BANDS):
         for xh in range(2):
             at = (band * 2 + xh) * RUN
-            out_ref[band % 2 * 2 + xh, band // 2] = cross[at : at + RUN]
+            out_ref[(band % 2 * 2 + xh) ^ NARROW, band // 2] = cross[at : at + RUN]
 
 
 def middle_kernel(kept_ref, got_ref, cross_ref, out_ref):
-    for at, zo in enumerate(QUARTERS):
-        out_ref[at, 0] = kept_ref[zo] + got_ref[zo]
-        out_ref[at, 1] = cross_ref[0, zo] + cross_ref[1, zo] + cross_ref[2, zo] + cross_ref[3, zo]
+    for zo in range(4):
+        out_ref[zo ^ WIDE, 0] = kept_ref[zo] + got_ref[zo]
+        out_ref[zo ^ WIDE, 1] = cross_ref[0, zo] + cross_ref[1, zo] + cross_ref[2, zo] + cross_ref[3, zo]
 
 
 def total_kernel(terms_ref, self_ref, cross_ref):
@@ -155,10 +160,10 @@
 
 def local(grads, partner):
     own = grads[0]
-    chunks = lax.all_to_all(own.reshape(GROUPS, BAND, FEATS), "grp", 0, 0)
+    chunks = exchange(own.reshape(GROUPS, BAND, FEATS), "grp", FIRST)
     above = lax.ppermute(own, "zl", SWAP)
-    routed = call(route_kernel, (GROUPS * QUAD, 2, RUN, FEATS), [SMEM, VMEM], (partner, chunks), 8)
-    mate = lax.all_to_all(routed, ("grp", "zl", "core"), 0, 0)
+    routed = call(route_kernel, (GROUPS * QUAD, 2, RUN, FEATS), [VMEM, VMEM], (partner, chunks), 8)
+    mate = exchange(routed, ("grp", "zl", "core"), SECOND)
     near = call(stack_kernel, (2, ROWS, FEATS), [VMEM, VMEM], (own, above), 8)
     cores = lax.ppermute(near, "core", SWAP)
     scratch = [pltpu.VMEM((MINE, FEATS), jnp.float32)]
@@ -167,11 +172,11 @@
     kept, sent = call(half_kernel, [some] * 2, [VMEM, VMEM], (kept, lax.ppermute(sent, "zm", SWAP)), 8, 2 * HINT)
     got = lax.ppermute(sent, "xh", SWAP)
     cross = call(
-        cross_kernel, (4, 4, RUN, ROWS), [SMEM] + [VMEM] * 3, (partner, near, cores, mate), 12, 0, scratch
+        cross_kernel, (4, 4, RUN, ROWS), [VMEM] * 4, (partner, near, cores, mate), 12, 0, scratch
     )
-    cross = lax.all_to_all(cross, ("zm", "xh"), 0, 0)
+    cross = exchange(cross, ("zm", "xh"), NARROW)
     terms = call(middle_kernel, (4, 2, RUN, ROWS), [VMEM] * 3, (kept, got, cross), 8)
-    terms = lax.all_to_all(terms, "zo", 0, 0, axis_index_groups=[list(QUARTERS)])
+    terms = exchange(terms, "zo", WIDE)
     return tuple(call(total_kernel, [(1, RUN, ROWS)] * 2, [VMEM], (terms,), 8))
 
 

time: 73 us -> 71 us (0.973)
  the two profiles are of different devices: /device:TPU:1 before, /device:TPU:6 now
where the time goes in v5:
time: 71 us; the launch traced here: 70.5 us
  starting transfers between devices  33.3 us (47%)
  blocking collectives  20 us (28%)
  waiting for transfers between devices  12.2 us (17%)
  Pallas kernels  4.17 us (6%)
  between operations  0.73 us (1%)
    all_to_all x1, blocking collectives, exchange(): return lax.all_to_all(values, axes, 0, 0, axis_index_groups=[members])  20 us
    all_to_all x3, starting transfers between devices, exchange(): return lax.all_to_all(values, axes, 0, 0, axis_index_groups=[members])  18.3 us
    ppermute x1, starting transfers between devices, local(): lax.ppermute(sent, 'zm', SWAP)  5.18 us
    all_to_all x3, waiting for transfers between devices, exchange(): return lax.all_to_all(values, axes, 0, 0, axis_index_groups=[members])  4.35 us
    pallas_call x7, Pallas kernels, call(): pl.pallas_call(kernel, out_shape=[one(dims) for dims in shape] if several...  4.17 us
    ppermute x1, starting transfers between devices, local(): above = lax.ppermute(own, 'zl', SWAP)  3.95 us
    ppermute x1, starting transfers between devices, local(): got = lax.ppermute(sent, 'xh', SWAP)  3.85 us
    ppermute x1, waiting for transfers between devices, local(): got = lax.ppermute(sent, 'xh', SWAP)  3.81 us
  transfers between devices with their start and end apart: 7, of which 5 were waited for; matrix products, arithmetic and copies ran while one was open for 0% of the time, Pallas kernels for 5%

profile of v5, /device:TPU:6, one launch (start us, length us, event | category | flops | bytes accessed | tf_op | source)
XLA Modules:
  0.0 70.5 jit_solution(15799590117578758502)
XLA Ops:
  0.6 0.0 copy-start
  0.6 7.0 %all-to-all-start = ((f32[8,64,256]{2,1,0:T(8,128)}), f32[8,64,256]{2,1,0:T(8,128)S(1)}, u32[]{:S(2)}, u32[]{:S(2)}) async-start(f32[8,64,256]{2,1,0:T(8,128)} %bitcast.2), calls=%async_computation | async-start | bytes 1048576 | tf_op jit(solution)/shard_map/all_to_all | solution.py:28
  7.7 0.0 copy-start.1
  7.7 0.0 copy-done
  7.7 4.0 %collective-permute-start = (f32[512,256]{1,0:T(8,128)S(1)}, f32[512,256]{1,0:T(8,128)S(1)}, u32[]{:S(2)}, u32[]{:S(2)}) collective-permute-start(f32[512,256]{1,0:T(8,128)S(1)} %bitcast.3), channel_id=1, source_target_pairs={{0,4},{4,0},{1,5},{5,1},{2,6},{6,2},{3,7},{7,3},{8,12},{12,8},{9,1... | collective-permute-start | bytes 1572872 | tf_op jit(solution)/shard_map/ppermute | solution.py:164
  11.6 0.0 copy-done.1
  11.6 0.1 copy.5.partner_ref
  11.7 2.7 %all-to-all-done.rows_ref = f32[8,64,256]{2,1,0:T(8,128)S(1)} async-done(((f32[8,64,256]{2,1,0:T(8,128)}), f32[8,64,256]{2,1,0:T(8,128)S(1)}, u32[]{:S(2)}, u32[]{:S(2)}) %all-to-all-start) | async-done | bytes 524320 | tf_op jit(solution)/shard_map/all_to_all | solution.py:28
  14.4 1.0 %route_kernel.1 = f32[32,2,8,256]{3,2,1,0:T(8,128)} custom-call(s32[8,2]{1,0:T(8,128)S(1)} %copy.5.partner_ref, f32[8,64,256]{2,1,0:T(8,128)S(1)} %all-to-all-done.rows_ref), custom_call_target="tpu_custom_call" | custom-call | tf_op jit(solution)/shard_map/route_kernel/pallas_call | solution.py:36
  15.4 7.8 %all-to-all-start.1 = ((f32[32,2,8,256]{3,2,1,0:T(8,128)}), f32[32,2,8,256]{3,2,1,0:T(8,128)S(1)}, u32[]{:S(2)}, u32[]{:S(2)}) async-start(f32[32,2,8,256]{3,2,1,0:T(8,128)} %route_kernel.1), calls=%async_computation.1 | async-start | bytes 1048576 | tf_op jit(solution)/shard_map/all_to_all | solution.py:28
  23.3 0.0 collective-permute-done.above_ref
  23.3 0.1 stack_kernel.1.near_ref
  23.4 2.1 %collective-permute-start.1 = (f32[2,512,256]{2,1,0:T(8,128)S(1)}, f32[2,512,256]{2,1,0:T(8,128)S(1)}, u32[]{:S(2)}, u32[]{:S(2)}) collective-permute-start(f32[2,512,256]{2,1,0:T(8,128)S(1)} %stack_kernel.1.near_ref), channel_id=1, source_target_pairs={{0,1},{1,0},{2,3},{3,2},{4,5},{5,4},{6,7},{7,6},{8,9},{9,8},{10,11... | collective-permute-start | bytes 3145736 | tf_op jit(solution)/shard_map/ppermute | solution.py:168
  25.4 2.5 %collective-permute-done.1.cores_ref = f32[2,512,256]{2,1,0:T(8,128)S(1)} collective-permute-done((f32[2,512,256]{2,1,0:T(8,128)S(1)}, f32[2,512,256]{2,1,0:T(8,128)S(1)}, u32[]{:S(2)}, u32[]{:S(2)}) %collective-permute-start.1) | collective-permute-done | bytes 1048608 | tf_op jit(solution)/shard_map/ppermute | solution.py:168
  27.9 0.8 %self_kernel.1 = (f32[8,8,512]{2,1,0:T(8,128)S(1)}, f32[8,8,512]{2,1,0:T(8,128)S(1)}) custom-call(f32[2,512,256]{2,1,0:T(8,128)S(1)} %stack_kernel.1.near_ref, f32[2,512,256]{2,1,0:T(8,128)S(1)} %collective-permute-done.1.cores_ref), custom_call_target="tpu_custom_call" | custom-call | flops 5000000000 | tf_op jit(solution)/shard_map/self_kernel/pallas_call | solution.py:36
  28.7 5.2 %collective-permute-start.2 = (f32[8,8,512]{2,1,0:T(8,128)S(1)}, f32[8,8,512]{2,1,0:T(8,128)S(1)}, u32[]{:S(2)}, u32[]{:S(2)}) collective-permute-start(f32[8,8,512]{2,1,0:T(8,128)S(1)} %get-tuple-element.7), channel_id=1, source_target_pairs={{0,8},{8,0},{1,9},{9,1},{2,10},{10,2},{3,11},{11,3},{4,12},{12,4},... | collective-permute-start | bytes 393224 | tf_op jit(solution)/shard_map/ppermute | solution.py:172
  33.9 0.0 all-to-all-done.1.mate_ref
  33.9 1.6 %cross_kernel.1 = f32[4,4,8,512]{3,2,1,0:T(8,128)} custom-call(s32[8,2]{1,0:T(8,128)S(1)} %copy.5.partner_ref, f32[2,512,256]{2,1,0:T(8,128)S(1)} %stack_kernel.1.near_ref, f32[2,512,256]{2,1,0:T(8,128)S(1)} %collective-permute-done.1.cores_ref, f32[32,2,8,256]{3,2,1,0:T(8,128)S(1)} %all-to-all-done.1.mate_ref), custom_call_target="tpu_custom_call" | custom-call | tf_op jit(solution)/shard_map/cross_kernel/pallas_call | solution.py:36
  35.6 3.4 %all-to-all-start.2 = ((f32[4,4,8,512]{3,2,1,0:T(8,128)}), f32[4,4,8,512]{3,2,1,0:T(8,128)S(1)}, u32[]{:S(2)}, u32[]{:S(2)}) async-start(f32[4,4,8,512]{3,2,1,0:T(8,128)} %cross_kernel.1), calls=%async_computation.2 | async-start | bytes 524288 | tf_op jit(solution)/shard_map/all_to_all | solution.py:28
  39.0 1.6 %collective-permute-done.2.got_ref = f32[8,8,512]{2,1,0:T(8,128)S(1)} collective-permute-done((f32[8,8,512]{2,1,0:T(8,128)S(1)}, f32[8,8,512]{2,1,0:T(8,128)S(1)}, u32[]{:S(2)}, u32[]{:S(2)}) %collective-permute-start.2) | collective-permute-done | bytes 131104 | tf_op jit(solution)/shard_map/ppermute | solution.py:172
  40.6 3.9 %collective-permute-start.3 = (f32[4,8,512]{2,1,0:T(8,128)S(1)}, f32[4,8,512]{2,1,0:T(8,128)S(1)}, u32[]{:S(2)}, u32[]{:S(2)}) collective-permute-start(f32[4,8,512]{2,1,0:T(8,128)S(1)} %get-tuple-element.9), channel_id=1, source_target_pairs={{0,2},{2,0},{1,3},{3,1},{4,6},{6,4},{5,7},{7,5},{8,10},{10,8},{9,1... | collective-permute-start | bytes 196616 | tf_op jit(solution)/shard_map/ppermute | solution.py:173
  44.4 3.8 %collective-permute-done.3.got_ref = f32[4,8,512]{2,1,0:T(8,128)S(1)} collective-permute-done((f32[4,8,512]{2,1,0:T(8,128)S(1)}, f32[4,8,512]{2,1,0:T(8,128)S(1)}, u32[]{:S(2)}, u32[]{:S(2)}) %collective-permute-start.3) | collective-permute-done | bytes 65568 | tf_op jit(solution)/shard_map/ppermute | solution.py:173
  48.2 1.6 %all-to-all-done.2.cross_ref = f32[4,4,8,512]{3,2,1,0:T(8,128)S(1)} async-done(((f32[4,4,8,512]{3,2,1,0:T(8,128)}), f32[4,4,8,512]{3,2,1,0:T(8,128)S(1)}, u32[]{:S(2)}, u32[]{:S(2)}) %all-to-all-start.2) | async-done | bytes 262176 | tf_op jit(solution)/shard_map/all_to_all | solution.py:28
  49.9 20.0 %all_to_all.20.terms_ref = f32[4,2,8,512]{3,2,1,0:T(8,128)S(1)} all-to-all(f32[4,2,8,512]{3,2,1,0:T(8,128)S(1)} %middle_kernel.1), channel_id=1, replica_groups={{32,48,0,16},{33,49,1,17},{34,50,2,18},{35,51,3,19},{36,52,4,20},{37,53..., dimensions={0} | all-to-all | bytes 262144 | tf_op jit(solution)/shard_map/all_to_all | solution.py:28
  69.8 0.6 total_kernel.1
  (2 shorter events, 0.0 us)
Async XLA Ops:
  0.6 7.0 %copy-start = (f32[1,512,256]{2,1,0:T(8,128)S(1)}, f32[1,512,256]{2,1,0:T(8,128)}, u32[]{:S(2)}) copy-start(f32[1,512,256]{2,1,0:T(8,128)} %param.2) | copy-start | bytes 1572868
  0.6 13.8 %all-to-all-start = ((f32[8,64,256]{2,1,0:T(8,128)}), f32[8,64,256]{2,1,0:T(8,128)S(1)}, u32[]{:S(2)}, u32[]{:S(2)}) async-start(f32[8,64,256]{2,1,0:T(8,128)} %bitcast.2), calls=%async_computation | async-start | bytes 1048576 | tf_op jit(solution)/shard_map/all_to_all | solution.py:28
  7.7 4.0 %copy-start.1 = (s32[8,2]{0,1:T(2,128)S(1)}, s32[8,2]{0,1:T(2,128)}, u32[]{:S(2)}) copy-start(s32[8,2]{0,1:T(2,128)} %param.3) | copy-start | bytes 196
  7.7 15.6 %collective-permute-start = (f32[512,256]{1,0:T(8,128)S(1)}, f32[512,256]{1,0:T(8,128)S(1)}, u32[]{:S(2)}, u32[]{:S(2)}) collective-permute-start(f32[512,256]{1,0:T(8,128)S(1)} %bitcast.3), channel_id=1, source_target_pairs={{0,4},{4,0},{1,5},{5,1},{2,6},{6,2},{3,7},{7,3},{8,12},{12,8},{9,1... | collective-permute-start | bytes 1572872 | tf_op jit(solution)/shard_map/ppermute | solution.py:164
  15.4 18.5 %all-to-all-start.1 = ((f32[32,2,8,256]{3,2,1,0:T(8,128)}), f32[32,2,8,256]{3,2,1,0:T(8,128)S(1)}, u32[]{:S(2)}, u32[]{:S(2)}) async-start(f32[32,2,8,256]{3,2,1,0:T(8,128)} %route_kernel.1), calls=%async_computation.1 | async-start | bytes 1048576 | tf_op jit(solution)/shard_map/all_to_all | solution.py:28
  23.4 4.6 %collective-permute-start.1 = (f32[2,512,256]{2,1,0:T(8,128)S(1)}, f32[2,512,256]{2,1,0:T(8,128)S(1)}, u32[]{:S(2)}, u32[]{:S(2)}) collective-permute-start(f32[2,512,256]{2,1,0:T(8,128)S(1)} %stack_kernel.1.near_ref), channel_id=1, source_target_pairs={{0,1},{1,0},{2,3},{3,2},{4,5},{5,4},{6,7},{7,6},{8,9},{9,8},{10,11... | collective-permute-start | bytes 3145736 | tf_op jit(solution)/shard_map/ppermute | solution.py:168
  28.7 11.8 %collective-permute-start.2 = (f32[8,8,512]{2,1,0:T(8,128)S(1)}, f32[8,8,512]{2,1,0:T(8,128)S(1)}, u32[]{:S(2)}, u32[]{:S(2)}) collective-permute-start(f32[8,8,512]{2,1,0:T(8,128)S(1)} %get-tuple-element.7), channel_id=1, source_target_pairs={{0,8},{8,0},{1,9},{9,1},{2,10},{10,2},{3,11},{11,3},{4,12},{12,4},... | collective-permute-start | bytes 393224 | tf_op jit(solution)/shard_map/ppermute | solution.py:172
  35.6 14.3 %all-to-all-start.2 = ((f32[4,4,8,512]{3,2,1,0:T(8,128)}), f32[4,4,8,512]{3,2,1,0:T(8,128)S(1)}, u32[]{:S(2)}, u32[]{:S(2)}) async-start(f32[4,4,8,512]{3,2,1,0:T(8,128)} %cross_kernel.1), calls=%async_computation.2 | async-start | bytes 524288 | tf_op jit(solution)/shard_map/all_to_all | solution.py:28
  40.6 7.7 %collective-permute-start.3 = (f32[4,8,512]{2,1,0:T(8,128)S(1)}, f32[4,8,512]{2,1,0:T(8,128)S(1)}, u32[]{:S(2)}, u32[]{:S(2)}) collective-permute-start(f32[4,8,512]{2,1,0:T(8,128)S(1)} %get-tuple-element.9), channel_id=1, source_target_pairs={{0,2},{2,0},{1,3},{3,1},{4,6},{6,4},{5,7},{7,5},{8,10},{10,8},{9,1... | collective-permute-start | bytes 196616 | tf_op jit(solution)/shard_map/ppermute | solution.py:173

commit v6 on v5

--- a/solution.py
+++ b/solution.py
@@ -30,7 +30,7 @@
 
 def call(kernel, shape, specs, arrays, limit, flops=0, scratch=()):
     def one(dims):
-        return jax.ShapeDtypeStruct(dims, jnp.float32)
+        return dims if isinstance(dims, jax.ShapeDtypeStruct) else jax.ShapeDtypeStruct(dims, jnp.float32)
 
     several = isinstance(shape, list)
     return pl.pallas_call(
@@ -74,17 +74,14 @@
     return lax.dot_general(left, right, (((1,), (1,)), ((), ())), preferred_element_type=jnp.float32)
 
 
-def products(blocks, rows_ref, fill):
-    total = rest = None
-    for i, block in enumerate(blocks):
-        fill(i)
-        rows_high, rows_low = halves(rows_ref[...])
-        high, low = halves(block[...])
-        part = dot(high, jnp.concatenate([rows_high, rows_low], axis=0))
-        other = dot(low, rows_high)
-        total = part if total is None else total + part
-        rest = other if rest is None else rest + other
-    return (total[:, :MINE] + total[:, MINE:] + rest).T
+def products(high_ref, low_ref, rows_ref):
+    rows_high, rows_low = halves(rows_ref[...])
+    part = dot(high_ref[...], jnp.concatenate([rows_high, rows_low], axis=0))
+    return (part[:, :MINE] + part[:, MINE:] + dot(low_ref[...], rows_high)).T
+
+
+def columns(i):
+    return pl.ds(i * FEATS, FEATS)
 
 
 def blocks_of(near_ref, cores_ref):
@@ -95,19 +92,20 @@
     return lax.axis_index("zl") * 2 + lax.axis_index("core")
 
 
-def self_kernel(near_ref, cores_ref, keep_ref, send_ref, rows_ref):
+def self_kernel(near_ref, cores_ref, keep_ref, send_ref, high_ref, low_ref, rows_ref):
     me = member()
     zm = lax.axis_index("zm")
     blocks = blocks_of(near_ref, cores_ref)
 
-    def fill(i):
+    for i in range(QUAD):
+        high_ref[:, columns(i)], low_ref[:, columns(i)] = halves(blocks[i][...])
         for part in range(2):
             for at in range(BANDS):
                 band = at // 2 * 2 + (zm ^ part)
                 start = pl.multiple_of(band * BAND + run_of(me, at % 2) * RUN, RUN)
-                rows_ref[pl.ds((part * BANDS + at) * RUN, RUN), :] = blocks[i][pl.ds(start, RUN), :]
+                rows_ref[pl.ds((part * BANDS + at) * RUN, RUN), columns(i)] = blocks[i][pl.ds(start, RUN), :]
 
-    result = products(blocks, rows_ref, fill)
+    result = products(high_ref, low_ref, rows_ref)
     for band in range(BANDS):
         keep_ref[band] = result[band * RUN : (band + 1) * RUN]
         send_ref[band] = result[(BANDS + band) * RUN : (BANDS + band + 1) * RUN]
@@ -120,23 +118,23 @@
         send_ref[zo] = kept_ref[zo * 2 + 1 - xh] + got_ref[zo * 2 + 1 - xh]
 
 
-def cross_kernel(partner_ref, near_ref, cores_ref, mate_ref, out_ref, rows_ref):
+def cross_kernel(partner_ref, high_ref, low_ref, mate_ref, out_ref, rows_ref):
     me = member()
     offset = partner_ref[pl.ds(lax.axis_index("grp"), 1), :][0, 1]
     shift = offset // BAND
     row = lax.broadcasted_iota(jnp.int32, (RUN, FEATS), 0) + lax.rem(offset, BAND)
 
-    def fill(i):
+    for i in range(QUAD):
         source = me ^ NEAR[i]
         for band in range(BANDS):
             low = ((lax.rem(band + shift, BANDS) ^ FIRST) * QUAD + source) ^ SECOND
             high = ((lax.rem(band + shift + 1, BANDS) ^ FIRST) * QUAD + source) ^ SECOND
             for xh in range(2):
-                rows_ref[pl.ds((band * 2 + xh) * RUN, RUN), :] = jnp.where(
+                rows_ref[pl.ds((band * 2 + xh) * RUN, RUN), columns(i)] = jnp.where(
                     row + run_of(me, xh) * RUN >= BAND, mate_ref[high, xh], mate_ref[low, xh]
                 )
 
-    cross = products(blocks_of(near_ref, cores_ref), rows_ref, fill)
+    cross = products(high_ref, low_ref, rows_ref)
     for band in range(BANDS):
         for xh in range(2):
             at = (band * 2 + xh) * RUN
@@ -166,13 +164,14 @@
     mate = exchange(routed, ("grp", "zl", "core"), SECOND)
     near = call(stack_kernel, (2, ROWS, FEATS), [VMEM, VMEM], (own, above), 8)
     cores = lax.ppermute(near, "core", SWAP)
-    scratch = [pltpu.VMEM((MINE, FEATS), jnp.float32)]
+    scratch = [pltpu.VMEM((MINE, QUAD * FEATS), jnp.float32)]
     bands, some = (BANDS, RUN, ROWS), (4, RUN, ROWS)
-    kept, sent = call(self_kernel, [bands] * 2, [VMEM, VMEM], (near, cores), 12, HINT, scratch)
+    half = jax.ShapeDtypeStruct((ROWS, QUAD * FEATS), jnp.bfloat16)
+    kept, sent, high, low = call(self_kernel, [bands, bands, half, half], [VMEM, VMEM], (near, cores), 12, HINT, scratch)
     kept, sent = call(half_kernel, [some] * 2, [VMEM, VMEM], (kept, lax.ppermute(sent, "zm", SWAP)), 8, 2 * HINT)
     got = lax.ppermute(sent, "xh", SWAP)
     cross = call(
-        cross_kernel, (4, 4, RUN, ROWS), [VMEM] * 4, (partner, near, cores, mate), 12, 0, scratch
+        cross_kernel, (4, 4, RUN, ROWS), [VMEM] * 4, (partner, high, low, mate), 12, 0, scratch
     )
     cross = exchange(cross, ("zm", "xh"), NARROW)
     terms = call(middle_kernel, (4, 2, RUN, ROWS), [VMEM] * 3, (kept, got, cross), 8)

time: 71 us -> 71 us (level)
  no operation moved by 1% of the time
where the time goes in v6:
time: 71 us; the launch traced here: 70.5 us
  starting transfers between devices  33.3 us (47%)
  blocking collectives  20 us (28%)
  waiting for transfers between devices  12.2 us (17%)
  Pallas kernels  4.22 us (6%)
  between operations  0.73 us (1%)
    all_to_all x1, blocking collectives, exchange(): return lax.all_to_all(values, axes, 0, 0, axis_index_groups=[members])  20 us
    all_to_all x3, starting transfers between devices, exchange(): return lax.all_to_all(values, axes, 0, 0, axis_index_groups=[members])  18.3 us
    ppermute x1, starting transfers between devices, local(): lax.ppermute(sent, 'zm', SWAP)  5.18 us
    all_to_all x3, waiting for transfers between devices, exchange(): return lax.all_to_all(values, axes, 0, 0, axis_index_groups=[members])  4.35 us
    pallas_call x7, Pallas kernels, call(): pl.pallas_call(kernel, out_shape=[one(dims) for dims in shape] if several...  4.22 us
    ppermute x1, starting transfers between devices, local(): above = lax.ppermute(own, 'zl', SWAP)  3.95 us
    ppermute x1, waiting for transfers between devices, local(): got = lax.ppermute(sent, 'xh', SWAP)  3.83 us
    ppermute x1, starting transfers between devices, local(): got = lax.ppermute(sent, 'xh', SWAP)  3.83 us
  transfers between devices with their start and end apart: 7, of which 5 were waited for; matrix products, arithmetic and copies ran while one was open for 0% of the time, Pallas kernels for 5%

profile of v6, /device:TPU:6, one launch (start us, length us, event | category | flops | bytes accessed | tf_op | source)
XLA Modules:
  0.0 70.5 jit_solution(5580409920279971107)
XLA Ops:
  0.6 0.0 copy-start
  0.6 7.0 %all-to-all-start = ((f32[8,64,256]{2,1,0:T(8,128)}), f32[8,64,256]{2,1,0:T(8,128)S(1)}, u32[]{:S(2)}, u32[]{:S(2)}) async-start(f32[8,64,256]{2,1,0:T(8,128)} %bitcast.2), calls=%async_computation | async-start | bytes 1048576 | tf_op jit(solution)/shard_map/all_to_all | solution.py:28
  7.7 0.0 copy-start.1
  7.7 0.0 copy-done
  7.7 4.0 %collective-permute-start = (f32[512,256]{1,0:T(8,128)S(1)}, f32[512,256]{1,0:T(8,128)S(1)}, u32[]{:S(2)}, u32[]{:S(2)}) collective-permute-start(f32[512,256]{1,0:T(8,128)S(1)} %bitcast.3), channel_id=1, source_target_pairs={{0,4},{4,0},{1,5},{5,1},{2,6},{6,2},{3,7},{7,3},{8,12},{12,8},{9,1... | collective-permute-start | bytes 1572872 | tf_op jit(solution)/shard_map/ppermute | solution.py:162
  11.6 0.0 copy-done.1
  11.6 0.1 copy.5.partner_ref
  11.7 2.7 %all-to-all-done.rows_ref = f32[8,64,256]{2,1,0:T(8,128)S(1)} async-done(((f32[8,64,256]{2,1,0:T(8,128)}), f32[8,64,256]{2,1,0:T(8,128)S(1)}, u32[]{:S(2)}, u32[]{:S(2)}) %all-to-all-start) | async-done | bytes 524320 | tf_op jit(solution)/shard_map/all_to_all | solution.py:28
  14.4 1.0 %route_kernel.1 = f32[32,2,8,256]{3,2,1,0:T(8,128)} custom-call(s32[8,2]{1,0:T(8,128)S(1)} %copy.5.partner_ref, f32[8,64,256]{2,1,0:T(8,128)S(1)} %all-to-all-done.rows_ref), custom_call_target="tpu_custom_call" | custom-call | tf_op jit(solution)/shard_map/route_kernel/pallas_call | solution.py:36
  15.4 7.8 %all-to-all-start.1 = ((f32[32,2,8,256]{3,2,1,0:T(8,128)}), f32[32,2,8,256]{3,2,1,0:T(8,128)S(1)}, u32[]{:S(2)}, u32[]{:S(2)}) async-start(f32[32,2,8,256]{3,2,1,0:T(8,128)} %route_kernel.1), calls=%async_computation.1 | async-start | bytes 1048576 | tf_op jit(solution)/shard_map/all_to_all | solution.py:28
  23.3 0.0 collective-permute-done.above_ref
  23.3 0.1 stack_kernel.1.near_ref
  23.4 2.1 %collective-permute-start.1 = (f32[2,512,256]{2,1,0:T(8,128)S(1)}, f32[2,512,256]{2,1,0:T(8,128)S(1)}, u32[]{:S(2)}, u32[]{:S(2)}) collective-permute-start(f32[2,512,256]{2,1,0:T(8,128)S(1)} %stack_kernel.1.near_ref), channel_id=1, source_target_pairs={{0,1},{1,0},{2,3},{3,2},{4,5},{5,4},{6,7},{7,6},{8,9},{9,8},{10,11... | collective-permute-start | bytes 3145736 | tf_op jit(solution)/shard_map/ppermute | solution.py:166
  25.4 2.5 %collective-permute-done.1.cores_ref = f32[2,512,256]{2,1,0:T(8,128)S(1)} collective-permute-done((f32[2,512,256]{2,1,0:T(8,128)S(1)}, f32[2,512,256]{2,1,0:T(8,128)S(1)}, u32[]{:S(2)}, u32[]{:S(2)}) %collective-permute-start.1) | collective-permute-done | bytes 1048608 | tf_op jit(solution)/shard_map/ppermute | solution.py:166
  27.9 0.9 %self_kernel.1 = (f32[8,8,512]{2,1,0:T(8,128)S(1)}, f32[8,8,512]{2,1,0:T(8,128)S(1)}, bf16[512,1024]{1,0:T(8,128)(2,1)S(1)}, bf16[512,1024]{1,0:T(8,128)(2,1)S(1)}) custom-call(f32[2,512,256]{2,1,0:T(8,128)S(1)} %stack_kernel.1.near_ref, f32[2,512,256]{2,1,0:T(8,128)S(1)} %collective-permute-done.1.cores_ref), custom_call_target="tpu_custom_call" | custom-call | flops 5000000000 | tf_op jit(solution)/shard_map/self_kernel/pallas_call | solution.py:36
  28.8 5.2 %collective-permute-start.2 = (f32[8,8,512]{2,1,0:T(8,128)S(1)}, f32[8,8,512]{2,1,0:T(8,128)S(1)}, u32[]{:S(2)}, u32[]{:S(2)}) collective-permute-start(f32[8,8,512]{2,1,0:T(8,128)S(1)} %get-tuple-element.9), channel_id=1, source_target_pairs={{0,8},{8,0},{1,9},{9,1},{2,10},{10,2},{3,11},{11,3},{4,12},{12,4},... | collective-permute-start | bytes 393224 | tf_op jit(solution)/shard_map/ppermute | solution.py:171
  34.0 0.0 all-to-all-done.1.mate_ref
  34.0 1.6 %cross_kernel.1 = f32[4,4,8,512]{3,2,1,0:T(8,128)} custom-call(s32[8,2]{1,0:T(8,128)S(1)} %copy.5.partner_ref, bf16[512,1024]{1,0:T(8,128)(2,1)S(1)} %get-tuple-element.12.high_ref, bf16[512,1024]{1,0:T(8,128)(2,1)S(1)} %get-tuple-element.13.low_ref, f32[32,2,8,256]{3,2,1,0:T(8,128)S(1)} %all-to-all-done.1.mate_ref), custom_call_target="tpu_custom_call" | custom-call | tf_op jit(solution)/shard_map/cross_kernel/pallas_call | solution.py:36
  35.6 3.4 %all-to-all-start.2 = ((f32[4,4,8,512]{3,2,1,0:T(8,128)}), f32[4,4,8,512]{3,2,1,0:T(8,128)S(1)}, u32[]{:S(2)}, u32[]{:S(2)}) async-start(f32[4,4,8,512]{3,2,1,0:T(8,128)} %cross_kernel.1), calls=%async_computation.2 | async-start | bytes 524288 | tf_op jit(solution)/shard_map/all_to_all | solution.py:28
  39.0 1.6 %collective-permute-done.2.got_ref = f32[8,8,512]{2,1,0:T(8,128)S(1)} collective-permute-done((f32[8,8,512]{2,1,0:T(8,128)S(1)}, f32[8,8,512]{2,1,0:T(8,128)S(1)}, u32[]{:S(2)}, u32[]{:S(2)}) %collective-permute-start.2) | collective-permute-done | bytes 131104 | tf_op jit(solution)/shard_map/ppermute | solution.py:171
  40.6 3.8 %collective-permute-start.3 = (f32[4,8,512]{2,1,0:T(8,128)S(1)}, f32[4,8,512]{2,1,0:T(8,128)S(1)}, u32[]{:S(2)}, u32[]{:S(2)}) collective-permute-start(f32[4,8,512]{2,1,0:T(8,128)S(1)} %get-tuple-element.11), channel_id=1, source_target_pairs={{0,2},{2,0},{1,3},{3,1},{4,6},{6,4},{5,7},{7,5},{8,10},{10,8},{9,1... | collective-permute-start | bytes 196616 | tf_op jit(solution)/shard_map/ppermute | solution.py:172
  44.5 3.8 %collective-permute-done.3.got_ref = f32[4,8,512]{2,1,0:T(8,128)S(1)} collective-permute-done((f32[4,8,512]{2,1,0:T(8,128)S(1)}, f32[4,8,512]{2,1,0:T(8,128)S(1)}, u32[]{:S(2)}, u32[]{:S(2)}) %collective-permute-start.3) | collective-permute-done | bytes 65568 | tf_op jit(solution)/shard_map/ppermute | solution.py:172
  48.3 1.6 %all-to-all-done.2.cross_ref = f32[4,4,8,512]{3,2,1,0:T(8,128)S(1)} async-done(((f32[4,4,8,512]{3,2,1,0:T(8,128)}), f32[4,4,8,512]{3,2,1,0:T(8,128)S(1)}, u32[]{:S(2)}, u32[]{:S(2)}) %all-to-all-start.2) | async-done | bytes 262176 | tf_op jit(solution)/shard_map/all_to_all | solution.py:28
  49.9 20.0 %all_to_all.20.terms_ref = f32[4,2,8,512]{3,2,1,0:T(8,128)S(1)} all-to-all(f32[4,2,8,512]{3,2,1,0:T(8,128)S(1)} %middle_kernel.1), channel_id=1, replica_groups={{32,48,0,16},{33,49,1,17},{34,50,2,18},{35,51,3,19},{36,52,4,20},{37,53..., dimensions={0} | all-to-all | bytes 262144 | tf_op jit(solution)/shard_map/all_to_all | solution.py:28
  69.9 0.6 total_kernel.1
  (2 shorter events, 0.0 us)
Async XLA Ops:
  0.6 7.0 %copy-start = (f32[1,512,256]{2,1,0:T(8,128)S(1)}, f32[1,512,256]{2,1,0:T(8,128)}, u32[]{:S(2)}) copy-start(f32[1,512,256]{2,1,0:T(8,128)} %param.2) | copy-start | bytes 1572868
  0.6 13.8 %all-to-all-start = ((f32[8,64,256]{2,1,0:T(8,128)}), f32[8,64,256]{2,1,0:T(8,128)S(1)}, u32[]{:S(2)}, u32[]{:S(2)}) async-start(f32[8,64,256]{2,1,0:T(8,128)} %bitcast.2), calls=%async_computation | async-start | bytes 1048576 | tf_op jit(solution)/shard_map/all_to_all | solution.py:28
  7.7 4.0 %copy-start.1 = (s32[8,2]{0,1:T(2,128)S(1)}, s32[8,2]{0,1:T(2,128)}, u32[]{:S(2)}) copy-start(s32[8,2]{0,1:T(2,128)} %param.3) | copy-start | bytes 196
  7.7 15.6 %collective-permute-start = (f32[512,256]{1,0:T(8,128)S(1)}, f32[512,256]{1,0:T(8,128)S(1)}, u32[]{:S(2)}, u32[]{:S(2)}) collective-permute-start(f32[512,256]{1,0:T(8,128)S(1)} %bitcast.3), channel_id=1, source_target_pairs={{0,4},{4,0},{1,5},{5,1},{2,6},{6,2},{3,7},{7,3},{8,12},{12,8},{9,1... | collective-permute-start | bytes 1572872 | tf_op jit(solution)/shard_map/ppermute | solution.py:162
  15.4 18.5 %all-to-all-start.1 = ((f32[32,2,8,256]{3,2,1,0:T(8,128)}), f32[32,2,8,256]{3,2,1,0:T(8,128)S(1)}, u32[]{:S(2)}, u32[]{:S(2)}) async-start(f32[32,2,8,256]{3,2,1,0:T(8,128)} %route_kernel.1), calls=%async_computation.1 | async-start | bytes 1048576 | tf_op jit(solution)/shard_map/all_to_all | solution.py:28
  23.4 4.6 %collective-permute-start.1 = (f32[2,512,256]{2,1,0:T(8,128)S(1)}, f32[2,512,256]{2,1,0:T(8,128)S(1)}, u32[]{:S(2)}, u32[]{:S(2)}) collective-permute-start(f32[2,512,256]{2,1,0:T(8,128)S(1)} %stack_kernel.1.near_ref), channel_id=1, source_target_pairs={{0,1},{1,0},{2,3},{3,2},{4,5},{5,4},{6,7},{7,6},{8,9},{9,8},{10,11... | collective-permute-start | bytes 3145736 | tf_op jit(solution)/shard_map/ppermute | solution.py:166
  28.8 11.8 %collective-permute-start.2 = (f32[8,8,512]{2,1,0:T(8,128)S(1)}, f32[8,8,512]{2,1,0:T(8,128)S(1)}, u32[]{:S(2)}, u32[]{:S(2)}) collective-permute-start(f32[8,8,512]{2,1,0:T(8,128)S(1)} %get-tuple-element.9), channel_id=1, source_target_pairs={{0,8},{8,0},{1,9},{9,1},{2,10},{10,2},{3,11},{11,3},{4,12},{12,4},... | collective-permute-start | bytes 393224 | tf_op jit(solution)/shard_map/ppermute | solution.py:171
  35.6 14.3 %all-to-all-start.2 = ((f32[4,4,8,512]{3,2,1,0:T(8,128)}), f32[4,4,8,512]{3,2,1,0:T(8,128)S(1)}, u32[]{:S(2)}, u32[]{:S(2)}) async-start(f32[4,4,8,512]{3,2,1,0:T(8,128)} %cross_kernel.1), calls=%async_computation.2 | async-start | bytes 524288 | tf_op jit(solution)/shard_map/all_to_all | solution.py:28
  40.6 7.7 %collective-permute-start.3 = (f32[4,8,512]{2,1,0:T(8,128)S(1)}, f32[4,8,512]{2,1,0:T(8,128)S(1)}, u32[]{:S(2)}, u32[]{:S(2)}) collective-permute-start(f32[4,8,512]{2,1,0:T(8,128)S(1)} %get-tuple-element.11), channel_id=1, source_target_pairs={{0,2},{2,0},{1,3},{3,1},{4,6},{6,4},{5,7},{7,5},{8,10},{10,8},{9,1... | collective-permute-start | bytes 196616 | tf_op jit(solution)/shard_map/ppermute | solution.py:172

commit v7 on v6

--- a/solution.py
+++ b/solution.py
@@ -19,7 +19,8 @@
 SWAP = [(0, 1), (1, 0)]
 NEAR = (0, 2, 1, 3)
 HINT = 5_000_000_000
-FIRST, SECOND, NARROW, WIDE = 4, 16, 1, 2
+FIRST, SECOND = 4, 16
+NARROW, WIDE = (1, 3, 0, 2), (2, 0, 1, 3)
 VMEM = pl.BlockSpec(memory_space=pltpu.VMEM)
 
 
@@ -138,13 +139,13 @@
     for band in range(BANDS):
         for xh in range(2):
             at = (band * 2 + xh) * RUN
-            out_ref[(band % 2 * 2 + xh) ^ NARROW, band // 2] = cross[at : at + RUN]
+            out_ref[NARROW.index(band % 2 * 2 + xh), band // 2] = cross[at : at + RUN]
 
 
 def middle_kernel(kept_ref, got_ref, cross_ref, out_ref):
     for zo in range(4):
-        out_ref[zo ^ WIDE, 0] = kept_ref[zo] + got_ref[zo]
-        out_ref[zo ^ WIDE, 1] = cross_ref[0, zo] + cross_ref[1, zo] + cross_ref[2, zo] + cross_ref[3, zo]
+        out_ref[WIDE.index(zo), 0] = kept_ref[zo] + got_ref[zo]
+        out_ref[WIDE.index(zo), 1] = cross_ref[0, zo] + cross_ref[1, zo] + cross_ref[2, zo] + cross_ref[3, zo]
 
 
 def total_kernel(terms_ref, self_ref, cross_ref):
@@ -173,9 +174,9 @@
     cross = call(
         cross_kernel, (4, 4, RUN, ROWS), [VMEM] * 4, (partner, high, low, mate), 12, 0, scratch
     )
-    cross = exchange(cross, ("zm", "xh"), NARROW)
+    cross = lax.all_to_all(cross, ("zm", "xh"), 0, 0, axis_index_groups=[list(NARROW)])
     terms = call(middle_kernel, (4, 2, RUN, ROWS), [VMEM] * 3, (kept, got, cross), 8)
-    terms = exchange(terms, "zo", WIDE)
+    terms = lax.all_to_all(terms, "zo", 0, 0, axis_index_groups=[list(WIDE)])
     return tuple(call(total_kernel, [(1, RUN, ROWS)] * 2, [VMEM], (terms,), 8))
 
 

time: 71 us -> 71.1 us (level)
    all_to_all x0 -> x1, starting transfers between devices: none -> 3.4 us  [local(): lax.all_to_all(cross, ('zm', 'xh'), 0, 0, axis_index_groups=[list(NARROW)])]
    all_to_all x3 -> x2, starting transfers between devices: 18.3 us -> 14.9 us  [exchange(): return lax.all_to_all(values, axes, 0, 0, axis_index_groups=[members])]
    all_to_all x0 -> x1, waiting for transfers between devices: none -> 1.62 us  [local(): lax.all_to_all(cross, ('zm', 'xh'), 0, 0, axis_index_groups=[list(NARROW)])]
    all_to_all x3 -> x2, waiting for transfers between devices: 4.35 us -> 2.73 us  [exchange(): return lax.all_to_all(values, axes, 0, 0, axis_index_groups=[members])]
where the time goes in v7:
time: 71.1 us; the launch traced here: 70.3 us
  starting transfers between devices  33.3 us (47%)
  blocking collectives  19.7 us (28%)
  waiting for transfers between devices  12.2 us (17%)
  Pallas kernels  4.22 us (6%)
  between operations  0.73 us (1%)
    all_to_all x1, blocking collectives, local(): terms = lax.all_to_all(terms, 'zo', 0, 0, axis_index_groups=[list(WIDE)])  19.7 us
    all_to_all x2, starting transfers between devices, exchange(): return lax.all_to_all(values, axes, 0, 0, axis_index_groups=[members])  14.9 us
    ppermute x1, starting transfers between devices, local(): lax.ppermute(sent, 'zm', SWAP)  5.18 us
    pallas_call x7, Pallas kernels, call(): pl.pallas_call(kernel, out_shape=[one(dims) for dims in shape] if several...  4.22 us
    ppermute x1, starting transfers between devices, local(): above = lax.ppermute(own, 'zl', SWAP)  3.95 us
    ppermute x1, starting transfers between devices, local(): got = lax.ppermute(sent, 'xh', SWAP)  3.83 us
    ppermute x1, waiting for transfers between devices, local(): got = lax.ppermute(sent, 'xh', SWAP)  3.83 us
    all_to_all x1, starting transfers between devices, local(): lax.all_to_all(cross, ('zm', 'xh'), 0, 0, axis_index_groups=[list(NARROW)])  3.4 us
  transfers between devices with their start and end apart: 7, of which 5 were waited for; matrix products, arithmetic and copies ran while one was open for 0% of the time, Pallas kernels for 5%

profile of v7, /device:TPU:6, one launch (start us, length us, event | category | flops | bytes accessed | tf_op | source)
XLA Modules:
  0.0 70.3 jit_solution(5998916134523267757)
XLA Ops:
  0.6 0.0 copy-start
  0.6 7.0 %all-to-all-start = ((f32[8,64,256]{2,1,0:T(8,128)}), f32[8,64,256]{2,1,0:T(8,128)S(1)}, u32[]{:S(2)}, u32[]{:S(2)}) async-start(f32[8,64,256]{2,1,0:T(8,128)} %bitcast.2), calls=%async_computation | async-start | bytes 1048576 | tf_op jit(solution)/shard_map/all_to_all | solution.py:29
  7.7 0.0 copy-start.1
  7.7 0.0 copy-done
  7.7 4.0 %collective-permute-start = (f32[512,256]{1,0:T(8,128)S(1)}, f32[512,256]{1,0:T(8,128)S(1)}, u32[]{:S(2)}, u32[]{:S(2)}) collective-permute-start(f32[512,256]{1,0:T(8,128)S(1)} %bitcast.3), channel_id=1, source_target_pairs={{0,4},{4,0},{1,5},{5,1},{2,6},{6,2},{3,7},{7,3},{8,12},{12,8},{9,1... | collective-permute-start | bytes 1572872 | tf_op jit(solution)/shard_map/ppermute | solution.py:163
  11.6 0.0 copy-done.1
  11.6 0.1 copy.5.partner_ref
  11.7 2.7 %all-to-all-done.rows_ref = f32[8,64,256]{2,1,0:T(8,128)S(1)} async-done(((f32[8,64,256]{2,1,0:T(8,128)}), f32[8,64,256]{2,1,0:T(8,128)S(1)}, u32[]{:S(2)}, u32[]{:S(2)}) %all-to-all-start) | async-done | bytes 524320 | tf_op jit(solution)/shard_map/all_to_all | solution.py:29
  14.4 1.0 %route_kernel.1 = f32[32,2,8,256]{3,2,1,0:T(8,128)} custom-call(s32[8,2]{1,0:T(8,128)S(1)} %copy.5.partner_ref, f32[8,64,256]{2,1,0:T(8,128)S(1)} %all-to-all-done.rows_ref), custom_call_target="tpu_custom_call" | custom-call | tf_op jit(solution)/shard_map/route_kernel/pallas_call | solution.py:37
  15.4 7.8 %all-to-all-start.1 = ((f32[32,2,8,256]{3,2,1,0:T(8,128)}), f32[32,2,8,256]{3,2,1,0:T(8,128)S(1)}, u32[]{:S(2)}, u32[]{:S(2)}) async-start(f32[32,2,8,256]{3,2,1,0:T(8,128)} %route_kernel.1), calls=%async_computation.1 | async-start | bytes 1048576 | tf_op jit(solution)/shard_map/all_to_all | solution.py:29
  23.3 0.0 collective-permute-done.above_ref
  23.3 0.1 stack_kernel.1.near_ref
  23.4 2.1 %collective-permute-start.1 = (f32[2,512,256]{2,1,0:T(8,128)S(1)}, f32[2,512,256]{2,1,0:T(8,128)S(1)}, u32[]{:S(2)}, u32[]{:S(2)}) collective-permute-start(f32[2,512,256]{2,1,0:T(8,128)S(1)} %stack_kernel.1.near_ref), channel_id=1, source_target_pairs={{0,1},{1,0},{2,3},{3,2},{4,5},{5,4},{6,7},{7,6},{8,9},{9,8},{10,11... | collective-permute-start | bytes 3145736 | tf_op jit(solution)/shard_map/ppermute | solution.py:167
  25.4 2.5 %collective-permute-done.1.cores_ref = f32[2,512,256]{2,1,0:T(8,128)S(1)} collective-permute-done((f32[2,512,256]{2,1,0:T(8,128)S(1)}, f32[2,512,256]{2,1,0:T(8,128)S(1)}, u32[]{:S(2)}, u32[]{:S(2)}) %collective-permute-start.1) | collective-permute-done | bytes 1048608 | tf_op jit(solution)/shard_map/ppermute | solution.py:167
  27.9 0.9 %self_kernel.1 = (f32[8,8,512]{2,1,0:T(8,128)S(1)}, f32[8,8,512]{2,1,0:T(8,128)S(1)}, bf16[512,1024]{1,0:T(8,128)(2,1)S(1)}, bf16[512,1024]{1,0:T(8,128)(2,1)S(1)}) custom-call(f32[2,512,256]{2,1,0:T(8,128)S(1)} %stack_kernel.1.near_ref, f32[2,512,256]{2,1,0:T(8,128)S(1)} %collective-permute-done.1.cores_ref), custom_call_target="tpu_custom_call" | custom-call | flops 5000000000 | tf_op jit(solution)/shard_map/self_kernel/pallas_call | solution.py:37
  28.8 5.2 %collective-permute-start.2 = (f32[8,8,512]{2,1,0:T(8,128)S(1)}, f32[8,8,512]{2,1,0:T(8,128)S(1)}, u32[]{:S(2)}, u32[]{:S(2)}) collective-permute-start(f32[8,8,512]{2,1,0:T(8,128)S(1)} %get-tuple-element.9), channel_id=1, source_target_pairs={{0,8},{8,0},{1,9},{9,1},{2,10},{10,2},{3,11},{11,3},{4,12},{12,4},... | collective-permute-start | bytes 393224 | tf_op jit(solution)/shard_map/ppermute | solution.py:172
  34.0 0.0 all-to-all-done.1.mate_ref
  34.0 1.6 %cross_kernel.1 = f32[4,4,8,512]{3,2,1,0:T(8,128)} custom-call(s32[8,2]{1,0:T(8,128)S(1)} %copy.5.partner_ref, bf16[512,1024]{1,0:T(8,128)(2,1)S(1)} %get-tuple-element.12.high_ref, bf16[512,1024]{1,0:T(8,128)(2,1)S(1)} %get-tuple-element.13.low_ref, f32[32,2,8,256]{3,2,1,0:T(8,128)S(1)} %all-to-all-done.1.mate_ref), custom_call_target="tpu_custom_call" | custom-call | tf_op jit(solution)/shard_map/cross_kernel/pallas_call | solution.py:37
  35.6 3.4 %all-to-all-start.2 = ((f32[4,4,8,512]{3,2,1,0:T(8,128)}), f32[4,4,8,512]{3,2,1,0:T(8,128)S(1)}, u32[]{:S(2)}, u32[]{:S(2)}) async-start(f32[4,4,8,512]{3,2,1,0:T(8,128)} %cross_kernel.1), calls=%async_computation.2 | async-start | bytes 524288 | tf_op jit(solution)/shard_map/all_to_all | solution.py:177
  39.0 1.6 %collective-permute-done.2.got_ref = f32[8,8,512]{2,1,0:T(8,128)S(1)} collective-permute-done((f32[8,8,512]{2,1,0:T(8,128)S(1)}, f32[8,8,512]{2,1,0:T(8,128)S(1)}, u32[]{:S(2)}, u32[]{:S(2)}) %collective-permute-start.2) | collective-permute-done | bytes 131104 | tf_op jit(solution)/shard_map/ppermute | solution.py:172
  40.6 3.8 %collective-permute-start.3 = (f32[4,8,512]{2,1,0:T(8,128)S(1)}, f32[4,8,512]{2,1,0:T(8,128)S(1)}, u32[]{:S(2)}, u32[]{:S(2)}) collective-permute-start(f32[4,8,512]{2,1,0:T(8,128)S(1)} %get-tuple-element.11), channel_id=1, source_target_pairs={{0,2},{2,0},{1,3},{3,1},{4,6},{6,4},{5,7},{7,5},{8,10},{10,8},{9,1... | collective-permute-start | bytes 196616 | tf_op jit(solution)/shard_map/ppermute | solution.py:173
  44.5 3.8 %collective-permute-done.3.got_ref = f32[4,8,512]{2,1,0:T(8,128)S(1)} collective-permute-done((f32[4,8,512]{2,1,0:T(8,128)S(1)}, f32[4,8,512]{2,1,0:T(8,128)S(1)}, u32[]{:S(2)}, u32[]{:S(2)}) %collective-permute-start.3) | collective-permute-done | bytes 65568 | tf_op jit(solution)/shard_map/ppermute | solution.py:173
  48.3 1.6 %all-to-all-done.2.cross_ref = f32[4,4,8,512]{3,2,1,0:T(8,128)S(1)} async-done(((f32[4,4,8,512]{3,2,1,0:T(8,128)}), f32[4,4,8,512]{3,2,1,0:T(8,128)S(1)}, u32[]{:S(2)}, u32[]{:S(2)}) %all-to-all-start.2) | async-done | bytes 262176 | tf_op jit(solution)/shard_map/all_to_all | solution.py:177
  49.9 19.7 %all_to_all.20.terms_ref = f32[4,2,8,512]{3,2,1,0:T(8,128)S(1)} all-to-all(f32[4,2,8,512]{3,2,1,0:T(8,128)S(1)} %middle_kernel.1), channel_id=1, replica_groups={{32,0,16,48},{33,1,17,49},{34,2,18,50},{35,3,19,51},{36,4,20,52},{37,5,..., dimensions={0} | all-to-all | bytes 262144 | tf_op jit(solution)/shard_map/all_to_all | solution.py:179
  69.7 0.6 total_kernel.1
  (2 shorter events, 0.0 us)
Async XLA Ops:
  0.6 7.0 %copy-start = (f32[1,512,256]{2,1,0:T(8,128)S(1)}, f32[1,512,256]{2,1,0:T(8,128)}, u32[]{:S(2)}) copy-start(f32[1,512,256]{2,1,0:T(8,128)} %param.2) | copy-start | bytes 1572868
  0.6 13.8 %all-to-all-start = ((f32[8,64,256]{2,1,0:T(8,128)}), f32[8,64,256]{2,1,0:T(8,128)S(1)}, u32[]{:S(2)}, u32[]{:S(2)}) async-start(f32[8,64,256]{2,1,0:T(8,128)} %bitcast.2), calls=%async_computation | async-start | bytes 1048576 | tf_op jit(solution)/shard_map/all_to_all | solution.py:29
  7.7 4.0 %copy-start.1 = (s32[8,2]{0,1:T(2,128)S(1)}, s32[8,2]{0,1:T(2,128)}, u32[]{:S(2)}) copy-start(s32[8,2]{0,1:T(2,128)} %param.3) | copy-start | bytes 196
  7.7 15.6 %collective-permute-start = (f32[512,256]{1,0:T(8,128)S(1)}, f32[512,256]{1,0:T(8,128)S(1)}, u32[]{:S(2)}, u32[]{:S(2)}) collective-permute-start(f32[512,256]{1,0:T(8,128)S(1)} %bitcast.3), channel_id=1, source_target_pairs={{0,4},{4,0},{1,5},{5,1},{2,6},{6,2},{3,7},{7,3},{8,12},{12,8},{9,1... | collective-permute-start | bytes 1572872 | tf_op jit(solution)/shard_map/ppermute | solution.py:163
  15.4 18.5 %all-to-all-start.1 = ((f32[32,2,8,256]{3,2,1,0:T(8,128)}), f32[32,2,8,256]{3,2,1,0:T(8,128)S(1)}, u32[]{:S(2)}, u32[]{:S(2)}) async-start(f32[32,2,8,256]{3,2,1,0:T(8,128)} %route_kernel.1), calls=%async_computation.1 | async-start | bytes 1048576 | tf_op jit(solution)/shard_map/all_to_all | solution.py:29
  23.4 4.6 %collective-permute-start.1 = (f32[2,512,256]{2,1,0:T(8,128)S(1)}, f32[2,512,256]{2,1,0:T(8,128)S(1)}, u32[]{:S(2)}, u32[]{:S(2)}) collective-permute-start(f32[2,512,256]{2,1,0:T(8,128)S(1)} %stack_kernel.1.near_ref), channel_id=1, source_target_pairs={{0,1},{1,0},{2,3},{3,2},{4,5},{5,4},{6,7},{7,6},{8,9},{9,8},{10,11... | collective-permute-start | bytes 3145736 | tf_op jit(solution)/shard_map/ppermute | solution.py:167
  28.8 11.8 %collective-permute-start.2 = (f32[8,8,512]{2,1,0:T(8,128)S(1)}, f32[8,8,512]{2,1,0:T(8,128)S(1)}, u32[]{:S(2)}, u32[]{:S(2)}) collective-permute-start(f32[8,8,512]{2,1,0:T(8,128)S(1)} %get-tuple-element.9), channel_id=1, source_target_pairs={{0,8},{8,0},{1,9},{9,1},{2,10},{10,2},{3,11},{11,3},{4,12},{12,4},... | collective-permute-start | bytes 393224 | tf_op jit(solution)/shard_map/ppermute | solution.py:172
  35.6 14.3 %all-to-all-start.2 = ((f32[4,4,8,512]{3,2,1,0:T(8,128)}), f32[4,4,8,512]{3,2,1,0:T(8,128)S(1)}, u32[]{:S(2)}, u32[]{:S(2)}) async-start(f32[4,4,8,512]{3,2,1,0:T(8,128)} %cross_kernel.1), calls=%async_computation.2 | async-start | bytes 524288 | tf_op jit(solution)/shard_map/all_to_all | solution.py:177
  40.6 7.7 %collective-permute-start.3 = (f32[4,8,512]{2,1,0:T(8,128)S(1)}, f32[4,8,512]{2,1,0:T(8,128)S(1)}, u32[]{:S(2)}, u32[]{:S(2)}) collective-permute-start(f32[4,8,512]{2,1,0:T(8,128)S(1)} %get-tuple-element.11), channel_id=1, source_target_pairs={{0,2},{2,0},{1,3},{3,1},{4,6},{6,4},{5,7},{7,5},{8,10},{10,8},{9,1... | collective-permute-start | bytes 196616 | tf_op jit(solution)/shard_map/ppermute | solution.py:173

commit v8 on v6

--- a/solution.py
+++ b/solution.py
@@ -19,7 +19,7 @@
 SWAP = [(0, 1), (1, 0)]
 NEAR = (0, 2, 1, 3)
 HINT = 5_000_000_000
-FIRST, SECOND, NARROW, WIDE = 4, 16, 1, 2
+FIRST, SECOND, NARROW, WIDE = 6, 24, 1, 2
 VMEM = pl.BlockSpec(memory_space=pltpu.VMEM)
 
 

time: 71 us -> 70.9 us (level)
  starting transfers between devices: 33.3 us -> 32.3 us
  waiting for transfers between devices: 12.2 us -> 13.1 us
    all_to_all x3, starting transfers between devices: 18.3 us -> 17.3 us  [exchange(): return lax.all_to_all(values, axes, 0, 0, axis_index_groups=[members])]
    all_to_all x3, waiting for transfers between devices: 4.35 us -> 5.22 us  [exchange(): return lax.all_to_all(values, axes, 0, 0, axis_index_groups=[members])]
where the time goes in v8:
time: 70.9 us; the launch traced here: 70.4 us
  starting transfers between devices  32.3 us (46%)
  blocking collectives  20 us (28%)
  waiting for transfers between devices  13.1 us (18%)
  Pallas kernels  4.22 us (6%)
  between operations  0.73 us (1%)
    all_to_all x1, blocking collectives, exchange(): return lax.all_to_all(values, axes, 0, 0, axis_index_groups=[members])  20 us
    all_to_all x3, starting transfers between devices, exchange(): return lax.all_to_all(values, axes, 0, 0, axis_index_groups=[members])  17.3 us
    all_to_all x3, waiting for transfers between devices, exchange(): return lax.all_to_all(values, axes, 0, 0, axis_index_groups=[members])  5.22 us
    ppermute x1, starting transfers between devices, local(): lax.ppermute(sent, 'zm', SWAP)  5.18 us
    pallas_call x7, Pallas kernels, call(): pl.pallas_call(kernel, out_shape=[one(dims) for dims in shape] if several...  4.22 us
    ppermute x1, starting transfers between devices, local(): above = lax.ppermute(own, 'zl', SWAP)  3.95 us
    ppermute x1, waiting for transfers between devices, local(): got = lax.ppermute(sent, 'xh', SWAP)  3.83 us
    ppermute x1, starting transfers between devices, local(): got = lax.ppermute(sent, 'xh', SWAP)  3.83 us
  transfers between devices with their start and end apart: 7, of which 5 were waited for; matrix products, arithmetic and copies ran while one was open for 0% of the time, Pallas kernels for 5%

profile of v8, /device:TPU:6, one launch (start us, length us, event | category | flops | bytes accessed | tf_op | source)
XLA Modules:
  0.0 70.4 jit_solution(7339345911030425768)
XLA Ops:
  0.6 0.0 copy-start
  0.6 6.9 %all-to-all-start = ((f32[8,64,256]{2,1,0:T(8,128)}), f32[8,64,256]{2,1,0:T(8,128)S(1)}, u32[]{:S(2)}, u32[]{:S(2)}) async-start(f32[8,64,256]{2,1,0:T(8,128)} %bitcast.2), calls=%async_computation | async-start | bytes 1048576 | tf_op jit(solution)/shard_map/all_to_all | solution.py:28
  7.5 0.0 copy-start.1
  7.5 0.0 copy-done
  7.5 4.0 %collective-permute-start = (f32[512,256]{1,0:T(8,128)S(1)}, f32[512,256]{1,0:T(8,128)S(1)}, u32[]{:S(2)}, u32[]{:S(2)}) collective-permute-start(f32[512,256]{1,0:T(8,128)S(1)} %bitcast.3), channel_id=1, source_target_pairs={{0,4},{4,0},{1,5},{5,1},{2,6},{6,2},{3,7},{7,3},{8,12},{12,8},{9,1... | collective-permute-start | bytes 1572872 | tf_op jit(solution)/shard_map/ppermute | solution.py:162
  11.5 0.0 copy-done.1
  11.5 0.1 copy.5.partner_ref
  11.6 3.6 %all-to-all-done.rows_ref = f32[8,64,256]{2,1,0:T(8,128)S(1)} async-done(((f32[8,64,256]{2,1,0:T(8,128)}), f32[8,64,256]{2,1,0:T(8,128)S(1)}, u32[]{:S(2)}, u32[]{:S(2)}) %all-to-all-start) | async-done | bytes 524320 | tf_op jit(solution)/shard_map/all_to_all | solution.py:28
  15.2 1.0 %route_kernel.1 = f32[32,2,8,256]{3,2,1,0:T(8,128)} custom-call(s32[8,2]{1,0:T(8,128)S(1)} %copy.5.partner_ref, f32[8,64,256]{2,1,0:T(8,128)S(1)} %all-to-all-done.rows_ref), custom_call_target="tpu_custom_call" | custom-call | tf_op jit(solution)/shard_map/route_kernel/pallas_call | solution.py:36
  16.2 7.0 %all-to-all-start.1 = ((f32[32,2,8,256]{3,2,1,0:T(8,128)}), f32[32,2,8,256]{3,2,1,0:T(8,128)S(1)}, u32[]{:S(2)}, u32[]{:S(2)}) async-start(f32[32,2,8,256]{3,2,1,0:T(8,128)} %route_kernel.1), calls=%async_computation.1 | async-start | bytes 1048576 | tf_op jit(solution)/shard_map/all_to_all | solution.py:28
  23.2 0.0 collective-permute-done.above_ref
  23.2 0.1 stack_kernel.1.near_ref
  23.2 2.1 %collective-permute-start.1 = (f32[2,512,256]{2,1,0:T(8,128)S(1)}, f32[2,512,256]{2,1,0:T(8,128)S(1)}, u32[]{:S(2)}, u32[]{:S(2)}) collective-permute-start(f32[2,512,256]{2,1,0:T(8,128)S(1)} %stack_kernel.1.near_ref), channel_id=1, source_target_pairs={{0,1},{1,0},{2,3},{3,2},{4,5},{5,4},{6,7},{7,6},{8,9},{9,8},{10,11... | collective-permute-start | bytes 3145736 | tf_op jit(solution)/shard_map/ppermute | solution.py:166
  25.3 2.5 %collective-permute-done.1.cores_ref = f32[2,512,256]{2,1,0:T(8,128)S(1)} collective-permute-done((f32[2,512,256]{2,1,0:T(8,128)S(1)}, f32[2,512,256]{2,1,0:T(8,128)S(1)}, u32[]{:S(2)}, u32[]{:S(2)}) %collective-permute-start.1) | collective-permute-done | bytes 1048608 | tf_op jit(solution)/shard_map/ppermute | solution.py:166
  27.8 0.9 %self_kernel.1 = (f32[8,8,512]{2,1,0:T(8,128)S(1)}, f32[8,8,512]{2,1,0:T(8,128)S(1)}, bf16[512,1024]{1,0:T(8,128)(2,1)S(1)}, bf16[512,1024]{1,0:T(8,128)(2,1)S(1)}) custom-call(f32[2,512,256]{2,1,0:T(8,128)S(1)} %stack_kernel.1.near_ref, f32[2,512,256]{2,1,0:T(8,128)S(1)} %collective-permute-done.1.cores_ref), custom_call_target="tpu_custom_call" | custom-call | flops 5000000000 | tf_op jit(solution)/shard_map/self_kernel/pallas_call | solution.py:36
  28.7 5.2 %collective-permute-start.2 = (f32[8,8,512]{2,1,0:T(8,128)S(1)}, f32[8,8,512]{2,1,0:T(8,128)S(1)}, u32[]{:S(2)}, u32[]{:S(2)}) collective-permute-start(f32[8,8,512]{2,1,0:T(8,128)S(1)} %get-tuple-element.9), channel_id=1, source_target_pairs={{0,8},{8,0},{1,9},{9,1},{2,10},{10,2},{3,11},{11,3},{4,12},{12,4},... | collective-permute-start | bytes 393224 | tf_op jit(solution)/shard_map/ppermute | solution.py:171
  33.8 0.0 all-to-all-done.1.mate_ref
  33.9 1.6 %cross_kernel.1 = f32[4,4,8,512]{3,2,1,0:T(8,128)} custom-call(s32[8,2]{1,0:T(8,128)S(1)} %copy.5.partner_ref, bf16[512,1024]{1,0:T(8,128)(2,1)S(1)} %get-tuple-element.12.high_ref, bf16[512,1024]{1,0:T(8,128)(2,1)S(1)} %get-tuple-element.13.low_ref, f32[32,2,8,256]{3,2,1,0:T(8,128)S(1)} %all-to-all-done.1.mate_ref), custom_call_target="tpu_custom_call" | custom-call | tf_op jit(solution)/shard_map/cross_kernel/pallas_call | solution.py:36
  35.5 3.4 %all-to-all-start.2 = ((f32[4,4,8,512]{3,2,1,0:T(8,128)}), f32[4,4,8,512]{3,2,1,0:T(8,128)S(1)}, u32[]{:S(2)}, u32[]{:S(2)}) async-start(f32[4,4,8,512]{3,2,1,0:T(8,128)} %cross_kernel.1), calls=%async_computation.2 | async-start | bytes 524288 | tf_op jit(solution)/shard_map/all_to_all | solution.py:28
  38.9 1.6 %collective-permute-done.2.got_ref = f32[8,8,512]{2,1,0:T(8,128)S(1)} collective-permute-done((f32[8,8,512]{2,1,0:T(8,128)S(1)}, f32[8,8,512]{2,1,0:T(8,128)S(1)}, u32[]{:S(2)}, u32[]{:S(2)}) %collective-permute-start.2) | collective-permute-done | bytes 131104 | tf_op jit(solution)/shard_map/ppermute | solution.py:171
  40.5 3.8 %collective-permute-start.3 = (f32[4,8,512]{2,1,0:T(8,128)S(1)}, f32[4,8,512]{2,1,0:T(8,128)S(1)}, u32[]{:S(2)}, u32[]{:S(2)}) collective-permute-start(f32[4,8,512]{2,1,0:T(8,128)S(1)} %get-tuple-element.11), channel_id=1, source_target_pairs={{0,2},{2,0},{1,3},{3,1},{4,6},{6,4},{5,7},{7,5},{8,10},{10,8},{9,1... | collective-permute-start | bytes 196616 | tf_op jit(solution)/shard_map/ppermute | solution.py:172
  44.3 3.8 %collective-permute-done.3.got_ref = f32[4,8,512]{2,1,0:T(8,128)S(1)} collective-permute-done((f32[4,8,512]{2,1,0:T(8,128)S(1)}, f32[4,8,512]{2,1,0:T(8,128)S(1)}, u32[]{:S(2)}, u32[]{:S(2)}) %collective-permute-start.3) | collective-permute-done | bytes 65568 | tf_op jit(solution)/shard_map/ppermute | solution.py:172
  48.2 1.6 %all-to-all-done.2.cross_ref = f32[4,4,8,512]{3,2,1,0:T(8,128)S(1)} async-done(((f32[4,4,8,512]{3,2,1,0:T(8,128)}), f32[4,4,8,512]{3,2,1,0:T(8,128)S(1)}, u32[]{:S(2)}, u32[]{:S(2)}) %all-to-all-start.2) | async-done | bytes 262176 | tf_op jit(solution)/shard_map/all_to_all | solution.py:28
  49.8 20.0 %all_to_all.20.terms_ref = f32[4,2,8,512]{3,2,1,0:T(8,128)S(1)} all-to-all(f32[4,2,8,512]{3,2,1,0:T(8,128)S(1)} %middle_kernel.1), channel_id=1, replica_groups={{32,48,0,16},{33,49,1,17},{34,50,2,18},{35,51,3,19},{36,52,4,20},{37,53..., dimensions={0} | all-to-all | bytes 262144 | tf_op jit(solution)/shard_map/all_to_all | solution.py:28
  69.8 0.6 total_kernel.1
  (2 shorter events, 0.0 us)
Async XLA Ops:
  0.6 6.9 %copy-start = (f32[1,512,256]{2,1,0:T(8,128)S(1)}, f32[1,512,256]{2,1,0:T(8,128)}, u32[]{:S(2)}) copy-start(f32[1,512,256]{2,1,0:T(8,128)} %param.2) | copy-start | bytes 1572868
  0.6 14.5 %all-to-all-start = ((f32[8,64,256]{2,1,0:T(8,128)}), f32[8,64,256]{2,1,0:T(8,128)S(1)}, u32[]{:S(2)}, u32[]{:S(2)}) async-start(f32[8,64,256]{2,1,0:T(8,128)} %bitcast.2), calls=%async_computation | async-start | bytes 1048576 | tf_op jit(solution)/shard_map/all_to_all | solution.py:28
  7.5 4.0 %copy-start.1 = (s32[8,2]{0,1:T(2,128)S(1)}, s32[8,2]{0,1:T(2,128)}, u32[]{:S(2)}) copy-start(s32[8,2]{0,1:T(2,128)} %param.3) | copy-start | bytes 196
  7.5 15.7 %collective-permute-start = (f32[512,256]{1,0:T(8,128)S(1)}, f32[512,256]{1,0:T(8,128)S(1)}, u32[]{:S(2)}, u32[]{:S(2)}) collective-permute-start(f32[512,256]{1,0:T(8,128)S(1)} %bitcast.3), channel_id=1, source_target_pairs={{0,4},{4,0},{1,5},{5,1},{2,6},{6,2},{3,7},{7,3},{8,12},{12,8},{9,1... | collective-permute-start | bytes 1572872 | tf_op jit(solution)/shard_map/ppermute | solution.py:162
  16.2 17.7 %all-to-all-start.1 = ((f32[32,2,8,256]{3,2,1,0:T(8,128)}), f32[32,2,8,256]{3,2,1,0:T(8,128)S(1)}, u32[]{:S(2)}, u32[]{:S(2)}) async-start(f32[32,2,8,256]{3,2,1,0:T(8,128)} %route_kernel.1), calls=%async_computation.1 | async-start | bytes 1048576 | tf_op jit(solution)/shard_map/all_to_all | solution.py:28
  23.2 4.6 %collective-permute-start.1 = (f32[2,512,256]{2,1,0:T(8,128)S(1)}, f32[2,512,256]{2,1,0:T(8,128)S(1)}, u32[]{:S(2)}, u32[]{:S(2)}) collective-permute-start(f32[2,512,256]{2,1,0:T(8,128)S(1)} %stack_kernel.1.near_ref), channel_id=1, source_target_pairs={{0,1},{1,0},{2,3},{3,2},{4,5},{5,4},{6,7},{7,6},{8,9},{9,8},{10,11... | collective-permute-start | bytes 3145736 | tf_op jit(solution)/shard_map/ppermute | solution.py:166
  28.7 11.8 %collective-permute-start.2 = (f32[8,8,512]{2,1,0:T(8,128)S(1)}, f32[8,8,512]{2,1,0:T(8,128)S(1)}, u32[]{:S(2)}, u32[]{:S(2)}) collective-permute-start(f32[8,8,512]{2,1,0:T(8,128)S(1)} %get-tuple-element.9), channel_id=1, source_target_pairs={{0,8},{8,0},{1,9},{9,1},{2,10},{10,2},{3,11},{11,3},{4,12},{12,4},... | collective-permute-start | bytes 393224 | tf_op jit(solution)/shard_map/ppermute | solution.py:171
  35.5 14.3 %all-to-all-start.2 = ((f32[4,4,8,512]{3,2,1,0:T(8,128)}), f32[4,4,8,512]{3,2,1,0:T(8,128)S(1)}, u32[]{:S(2)}, u32[]{:S(2)}) async-start(f32[4,4,8,512]{3,2,1,0:T(8,128)} %cross_kernel.1), calls=%async_computation.2 | async-start | bytes 524288 | tf_op jit(solution)/shard_map/all_to_all | solution.py:28
  40.5 7.7 %collective-permute-start.3 = (f32[4,8,512]{2,1,0:T(8,128)S(1)}, f32[4,8,512]{2,1,0:T(8,128)S(1)}, u32[]{:S(2)}, u32[]{:S(2)}) collective-permute-start(f32[4,8,512]{2,1,0:T(8,128)S(1)} %get-tuple-element.11), channel_id=1, source_target_pairs={{0,2},{2,0},{1,3},{3,1},{4,6},{6,4},{5,7},{7,5},{8,10},{10,8},{9,1... | collective-permute-start | bytes 196616 | tf_op jit(solution)/shard_map/ppermute | solution.py:172
